TPU v7x, 32 devices: a whole 2x2x4 slice. The times are simulated.
32 devices in a mesh: lat: 8 (over z, x), lev: 4 (over y, core).
Axes of the slice: x: 2, y: 2, z: 4, core: 2. Of those that a mesh axis runs over, the one named last changes fastest.
Arguments:
- tokens: bfloat16 [2, 4, 16, 64, 1024], P(None, 'lev', 'lat'), may hold values from -40 to 40
- key_mask: int32 [2, 16], replicated, may hold values from 0 to 1, as said below
- w_qkv: bfloat16 [1024, 3072], replicated, may hold values from -0.1875 to 0.1875
- w_mix: bfloat16 [4, 1024, 1024], P('lev'), may hold values from -0.09375 to 0.09375
- level_scale: float32 [4, 1024], P('lev'), may hold values from 0.1 to 1.9
- cotangent: bfloat16 [2, 4, 16, 64, 1024], P(None, 'lev', 'lat'), may hold values from -6 to 6
Outputs:
- output: bfloat16 [2, 4, 16, 64, 1024], P(None, 'lev', 'lat')
- d_tokens: bfloat16 [2, 4, 16, 64, 1024], P(None, 'lev', 'lat')
- mix_grad: float32 [4, 1024, 1024], P('lev', 'lat')
Inputs may be any that keep to these rules, and one draw needn't show every extreme that they name: `key_mask`: each sample has 1 to 4 padded rows, all at the end of the latitude rows, and the rest real; some sample has exactly 4 padded rows.
All inputs are finite; a program needn't handle non-finite values.
Results may differ from a plain program's by a relative error of at most 0.015.
Values may be sent and summed in bfloat16 or wider, within the bound.
No kernel may reach another device: no remote copies, remote signals or barrier semaphores. Data moves between devices by JAX's collectives and lax.ppermute only.
A program may use at most 128 MiB of HBM per device.

v0:
```python
import functools
import math

import jax
import jax.numpy as jnp
from jax import lax
from jax.experimental import pallas as pl
from jax.experimental.pallas import tpu as pltpu
from jax.sharding import PartitionSpec as P

HEADS = 16
GROUP = 256

epsilon = 1e-06
score_scale = 0.25

F32 = jnp.float32
BF16 = jnp.bfloat16


def nn(a, b):
    return lax.dot_general(a, b, (((1,), (0,)), ((), ())), preferred_element_type=F32)


def nt(a, b):
    return lax.dot_general(a, b, (((1,), (1,)), ((), ())), preferred_element_type=F32)


def tn(a, b):
    return lax.dot_general(a, b, (((0,), (0,)), ((), ())), preferred_element_type=F32)


def block_mean(head_width):
    row = lax.broadcasted_iota(jnp.int32, (GROUP, GROUP), 0) // head_width
    col = lax.broadcasted_iota(jnp.int32, (GROUP, GROUP), 1) // head_width
    return jnp.where(row == col, 1.0 / head_width, 0.0).astype(BF16)


def params():
    return pltpu.CompilerParams(vmem_limit_bytes=36 * 1024 * 1024)


def half_cols(which, width):
    half = width // 2
    core = lax.axis_index("lev") % 2
    return pl.ds(pl.multiple_of((core ^ which) * half, half), half)


def call(kernel, name, out_shape, *operands):
    return pl.pallas_call(
        kernel, out_shape=out_shape, compiler_params=params(), name=name
    )(*operands)


def pack_kernel(tok_ref, cot_ref, gain_ref, tok_out, *cot_outs):
    batch, rows, parts, chunk, width = tok_ref.shape
    for b in range(batch):
        for q in range(parts):
            for r in range(rows):
                tok_out[b * parts + q, r * chunk : (r + 1) * chunk, :] = tok_ref[b, r, q]
    for s in range(2):
        cols = half_cols(s, width)
        gain = gain_ref[:, cols]
        for b in range(batch):
            for q in range(parts):
                for r in range(rows):
                    piece = cot_ref[b, r, q, :, cols].astype(F32)
                    cot_outs[s][b * parts + q, r * chunk : (r + 1) * chunk, :] = (
                        piece * gain
                    ).astype(BF16)


def pack(tokens, cot, gain):
    batch, rows, parts, chunk, width = tokens.shape
    shape = (batch * parts, rows * chunk)
    return call(
        pack_kernel,
        "pack",
        [jax.ShapeDtypeStruct(shape + (width,), BF16)]
        + [jax.ShapeDtypeStruct(shape + (width // 2,), BF16)] * 2,
        tokens,
        cot,
        gain,
    )


def output_kernel(tok_ref, gain_ref, own_ref, other_ref, out_ref):
    batch, rows, parts, chunk, width = tok_ref.shape
    for s, ref in enumerate((own_ref, other_ref)):
        cols = half_cols(s, width)
        gain = gain_ref[:, cols]
        for b in range(batch):
            for q in range(parts):
                for r in range(rows):
                    mixed = ref[b * parts + q, r * chunk : (r + 1) * chunk, :].astype(F32)
                    out_ref[b, r, q, :, cols] = (
                        tok_ref[b, r, q, :, cols].astype(F32) + gain * mixed
                    ).astype(BF16)


def make_output(tokens, gain, mixed):
    return call(
        output_kernel,
        "make_output",
        jax.ShapeDtypeStruct(tokens.shape, BF16),
        tokens,
        gain,
        *mixed,
    )


def gradient_kernel(cot_ref, back_ref, out_ref):
    batch, rows, parts, chunk, width = cot_ref.shape
    for b in range(batch):
        for q in range(parts):
            for r in range(rows):
                back = back_ref[b * parts + q, r * chunk : (r + 1) * chunk, :].astype(F32)
                out_ref[b, r, q] = (cot_ref[b, r, q].astype(F32) + back).astype(BF16)


def make_gradient(cot, back):
    return call(
        gradient_kernel, "make_gradient", jax.ShapeDtypeStruct(cot.shape, BF16), cot, back
    )


def forward_kernel(
    samples, lat_count, chunk, owners,
    tok_ref, mask_ref, wq_ref, wk_ref, wv_ref, wm_ref,
    qn_ref, kn_ref, v_ref, rq_ref, rk_ref, p_ref, att_ref, own_ref, other_ref,
    normed_ref, acc_ref, keep_ref,
):
    step = pl.program_id(0)
    count, width = normed_ref.shape
    head_width = width // HEADS

    @pl.when(step == 0)
    def _():
        x = tok_ref[...].astype(F32)
        rx = lax.rsqrt(jnp.mean(x * x, axis=-1, keepdims=True) + epsilon)
        normed_ref[...] = (x * rx).astype(BF16)
        acc_ref[...] = jnp.zeros_like(acc_ref)
        spread = (
            lax.broadcasted_iota(jnp.int32, (lat_count, count), 0)
            == lax.broadcasted_iota(jnp.int32, (lat_count, count), 1) // chunk
        ).astype(F32)
        per_sample = nn(mask_ref[...].astype(F32), spread)
        mine = lax.axis_index("lat") // (owners // samples)
        pick = lax.broadcasted_iota(jnp.int32, (samples, count), 0) == mine
        valid = jnp.sum(jnp.where(pick, per_sample, 0.0), axis=0, keepdims=True)
        same = (
            lax.broadcasted_iota(jnp.int32, (count, count), 0) % chunk
            == lax.broadcasted_iota(jnp.int32, (count, count), 1) % chunk
        )
        keep_ref[...] = jnp.where(same, valid, 0.0)

    normed = normed_ref[...]
    mean_mat = block_mean(head_width)
    q = nn(normed, wq_ref[...])
    k = nn(normed, wk_ref[...])
    v = nn(normed, wv_ref[...]).astype(BF16)
    rq = lax.rsqrt(nn((q * q).astype(BF16), mean_mat) + epsilon)
    rk = lax.rsqrt(nn((k * k).astype(BF16), mean_mat) + epsilon)
    qn = (q * rq).astype(BF16)
    kn = (k * rk).astype(BF16)
    qn_ref[...] = qn
    kn_ref[...] = kn
    v_ref[...] = v
    rq_ref[...] = rq
    rk_ref[...] = rk
    keep = keep_ref[...]
    lane = lax.broadcasted_iota(jnp.int32, (count, 128), 1) // head_width
    per_tile = 128 // head_width
    tiles = []
    for t in range(GROUP // 128):
        cols = slice(t * 128, (t + 1) * 128)
        q_t, k_t, v_t = qn[:, cols], kn[:, cols], v[:, cols]
        total = None
        for h in range(per_tile):
            q_h = jnp.where(lane == h, q_t * score_scale, jnp.zeros_like(q_t))
            e = jnp.exp(nt(q_h, k_t)) * keep
            p = (e * (1.0 / jnp.sum(e, axis=-1, keepdims=True))).astype(BF16)
            p_ref[t * per_tile + h] = p
            o = nn(p, v_t)
            total = o if total is None else jnp.where(lane == h, o, total)
        tiles.append(total)
    att = jnp.concatenate(tiles, axis=1).astype(BF16)
    features = att_ref.shape[-1]
    for f in range(GROUP // features):
        att_ref[f] = att[:, f * features : (f + 1) * features]
    acc_ref[...] += nn(att, wm_ref[...])

    @pl.when(step == pl.num_programs(0) - 1)
    def _():
        for s, ref in enumerate((own_ref, other_ref)):
            ref[...] = acc_ref[:, half_cols(s, width)].astype(BF16)


def forward(tok_col, key_mask, w_qkv, w_mix, chunk, owners):
    count, width = tok_col.shape
    samples, lat_count = key_mask.shape
    steps = width // GROUP
    per_step = GROUP // (width // HEADS)
    features = width // owners
    same = lambda shape: pl.BlockSpec(shape, lambda i: (0, 0))
    cols = pl.BlockSpec((count, GROUP), lambda i: (0, i))
    weight = lambda which: pl.BlockSpec((width, GROUP), lambda i: (0, i + which * steps))
    return pl.pallas_call(
        functools.partial(forward_kernel, samples, lat_count, chunk, owners),
        out_shape=(
            [jax.ShapeDtypeStruct((count, width), BF16)] * 3
            + [jax.ShapeDtypeStruct((count, width), F32)] * 2
            + [jax.ShapeDtypeStruct((HEADS, count, count), BF16)]
            + [jax.ShapeDtypeStruct((owners, count, features), BF16)]
            + [jax.ShapeDtypeStruct((count, width // 2), BF16)] * 2
        ),
        grid=(steps,),
        in_specs=[
            same((count, width)),
            same((samples, lat_count)),
            weight(0),
            weight(1),
            weight(2),
            pl.BlockSpec((GROUP, width), lambda i: (i, 0)),
        ],
        out_specs=(
            [cols] * 5
            + [pl.BlockSpec((per_step, count, count), lambda i: (i, 0, 0))]
            + [pl.BlockSpec((GROUP // features, count, features), lambda i: (i, 0, 0))]
            + [same((count, width // 2))] * 2
        ),
        scratch_shapes=[
            pltpu.VMEM((count, width), BF16),
            pltpu.VMEM((count, width), F32),
            pltpu.VMEM((count, count), F32),
        ],
        compiler_params=params(),
        cost_estimate=pl.CostEstimate(
            flops=2 * count * width * (4 * width + 2 * count * 4),
            bytes_accessed=20 * count * width + 8 * width * width,
            transcendentals=HEADS * count * count,
        ),
        name="forward",
    )(tok_col, key_mask, w_qkv, w_qkv, w_qkv, w_mix)


def backward_kernel(
    tok_ref, own_ref, other_ref, wm_ref, wq_ref, wk_ref, wv_ref,
    qn_ref, kn_ref, v_ref, rq_ref, rk_ref, p_ref,
    out_ref, acc_ref,
):
    step = pl.program_id(0)
    count, width = acc_ref.shape
    head_width = width // HEADS
    d_att = nt(own_ref[...], wm_ref[:, half_cols(0, width)])
    d_att += nt(other_ref[...], wm_ref[:, half_cols(1, width)])
    d_att = d_att.astype(BF16)
    qn, kn, v = qn_ref[...], kn_ref[...], v_ref[...]
    lane = lax.broadcasted_iota(jnp.int32, (count, 128), 1) // head_width
    per_tile = 128 // head_width
    dq_tiles, dk_tiles, dv_tiles = [], [], []
    for t in range(GROUP // 128):
        cols = slice(t * 128, (t + 1) * 128)
        q_t, k_t, v_t, d_t = qn[:, cols], kn[:, cols], v[:, cols], d_att[:, cols]
        dq = dk = dv = None
        for h in range(per_tile):
            d_h = jnp.where(lane == h, d_t, jnp.zeros_like(d_t))
            d_p = nt(d_h, v_t)
            p_b = p_ref[t * per_tile + h]
            p = p_b.astype(F32)
            pd = p * d_p
            d_s = ((pd - p * jnp.sum(pd, axis=-1, keepdims=True)) * score_scale).astype(BF16)
            dq_h, dk_h, dv_h = nn(d_s, k_t), tn(d_s, q_t), tn(p_b, d_t)
            if dq is None:
                dq, dk, dv = dq_h, dk_h, dv_h
            else:
                dq = jnp.where(lane == h, dq_h, dq)
                dk = jnp.where(lane == h, dk_h, dk)
                dv = jnp.where(lane == h, dv_h, dv)
        dq_tiles.append(dq)
        dk_tiles.append(dk)
        dv_tiles.append(dv)
    mean_mat = block_mean(head_width)
    dq = jnp.concatenate(dq_tiles, axis=1)
    dk = jnp.concatenate(dk_tiles, axis=1)
    dv = jnp.concatenate(dv_tiles, axis=1).astype(BF16)

    def through_norm(upstream, unit, factor):
        unit = unit.astype(F32)
        inner = nn((upstream * unit).astype(BF16), mean_mat)
        return (factor * (upstream - unit * inner)).astype(BF16)

    gq = through_norm(dq, qn, rq_ref[...])
    gk = through_norm(dk, kn, rk_ref[...])
    total = nt(gq, wq_ref[...]) + nt(gk, wk_ref[...]) + nt(dv, wv_ref[...])

    @pl.when(step == 0)
    def _():
        acc_ref[...] = total

    @pl.when(step > 0)
    def _():
        acc_ref[...] += total

    @pl.when(step == pl.num_programs(0) - 1)
    def _():
        x = tok_ref[...].astype(F32)
        rx = lax.rsqrt(jnp.mean(x * x, axis=-1, keepdims=True) + epsilon)
        d = acc_ref[...]
        inner = jnp.mean(d * x, axis=-1, keepdims=True)
        out_ref[...] = (rx * d - x * (rx * rx * rx * inner)).astype(BF16)


def backward(tok_col, flow, w_mix, w_qkv, saved):
    count, width = tok_col.shape
    steps = width // GROUP
    per_step = GROUP // (width // HEADS)
    same = lambda shape: pl.BlockSpec(shape, lambda i: (0, 0))
    cols = pl.BlockSpec((count, GROUP), lambda i: (0, i))
    weight = lambda which: pl.BlockSpec((width, GROUP), lambda i: (0, i + which * steps))
    return pl.pallas_call(
        backward_kernel,
        out_shape=jax.ShapeDtypeStruct((count, width), BF16),
        grid=(steps,),
        in_specs=[
            same((count, width)),
            same((count, width // 2)),
            same((count, width // 2)),
            pl.BlockSpec((GROUP, width), lambda i: (i, 0)),
            weight(0),
            weight(1),
            weight(2),
            *([cols] * 5),
            pl.BlockSpec((per_step, count, count), lambda i: (i, 0, 0)),
        ],
        out_specs=same((count, width)),
        scratch_shapes=[pltpu.VMEM((count, width), F32)],
        compiler_params=params(),
        cost_estimate=pl.CostEstimate(
            flops=2 * count * width * (4 * width + 4 * count * 4),
            bytes_accessed=20 * count * width + 8 * width * width,
            transcendentals=0,
        ),
        name="backward",
    )(tok_col, *flow, w_mix, w_qkv, w_qkv, w_qkv, *saved)


def mix_gradient_kernel(factor, own_ref, other_ref, flow_ref, own_out, other_out, flow_scr):
    bands, owners, cells, half = flow_ref.shape
    count = bands * cells
    features = own_ref.shape[-1]
    for j in range(owners):
        for p in range(bands):
            at = j * count + p * cells
            flow_scr[at : at + cells, :] = flow_ref[p, j]
    flow = flow_scr[...]
    own = own_ref[...].reshape(owners * count, features)
    other = other_ref[...].reshape(owners * count, features)
    own_out[...] = tn(own, flow) * factor
    other_out[...] = (tn(other, flow) * factor).astype(BF16)


def mix_gradient(own, other, flow_all, factor):
    owners, count, features = own.shape
    half = flow_all.shape[-1]
    return pl.pallas_call(
        functools.partial(mix_gradient_kernel, factor),
        out_shape=[
            jax.ShapeDtypeStruct((features, half), F32),
            jax.ShapeDtypeStruct((features, half), BF16),
        ],
        scratch_shapes=[pltpu.VMEM((owners * count, half), BF16)],
        compiler_params=params(),
        cost_estimate=pl.CostEstimate(
            flops=4 * owners * count * features * half,
            bytes_accessed=2 * owners * count * (2 * features + half),
            transcendentals=0,
        ),
        name="mix_gradient",
    )(own, other, flow_all)


def place_kernel(own_ref, other_ref, out_ref):
    width = out_ref.shape[-1]
    out_ref[:, half_cols(0, width)] = own_ref[...]
    out_ref[:, half_cols(1, width)] = other_ref[...].astype(F32)


def place(own, other):
    rows, half = own.shape
    return call(place_kernel, "place", jax.ShapeDtypeStruct((rows, 2 * half), F32), own, other)


def swap(block):
    return lax.all_to_all(block, "lat", split_axis=0, concat_axis=0, tiled=True)


def from_level(block, offset):
    return lax.ppermute(block, "lev", [(i, i ^ offset) for i in range(lax.axis_size("lev"))])


def level_total(own, other):
    total = own
    received = from_level(other, 1)
    offset = 1
    while True:
        total = (total.astype(F32) + received.astype(F32)).astype(BF16)
        offset *= 2
        if offset == lax.axis_size("lev"):
            return total
        received = from_level(total, offset)


def on_device(tokens, key_mask, w_qkv, w_mix, level_scale, cotangent):
    batch, _, rows, lon, width = tokens.shape
    owners = lax.axis_size("lat")
    parts = owners // batch
    chunk = lon // parts
    cells = rows * chunk
    count = batch * rows * lon
    half = width // 2
    tok_band = tokens.reshape(batch, rows, parts, chunk, width)
    cot_band = cotangent.reshape(batch, rows, parts, chunk, width)
    w_mix = w_mix.reshape(width, width)

    tok_send, cot_own, cot_other = pack(tok_band, cot_band, level_scale)
    tok_col = swap(tok_send).reshape(count, width)
    flow_band = level_total(cot_own, cot_other)
    flow_own = swap(flow_band).reshape(count, half)
    flow = (flow_own, from_level(flow_own, 1))
    flow_all = lax.all_gather(flow_band, "lat", axis=0)

    *saved, attended, mix_own, mix_other = forward(
        tok_col, key_mask, w_qkv, w_mix, chunk, owners
    )
    attended = swap(attended)
    mix_half = level_total(mix_own, mix_other)
    back_col = backward(tok_col, flow, w_mix, w_qkv, saved)
    back = swap(back_col.reshape(owners, cells, width))
    mix_band = swap(mix_half.reshape(owners, cells, half))
    output = make_output(tok_band, level_scale, (mix_band, from_level(mix_band, 1)))
    d_tokens = make_gradient(cot_band, back)

    factor = 1.0 / math.sqrt(count * owners)
    grad_own, grad_other = mix_gradient(attended, from_level(attended, 1), flow_all, factor)
    mix_grad = place(grad_own, from_level(grad_other, 1))
    return (
        output.reshape(tokens.shape),
        d_tokens.reshape(tokens.shape),
        mix_grad.reshape(1, width // owners, width),
    )


def solution(mesh):
    return jax.shard_map(
        on_device,
        mesh=mesh,
        in_specs=(
            P(None, "lev", "lat", None, None),
            P(),
            P(),
            P("lev", None, None),
            P("lev", None),
            P(None, "lev", "lat", None, None),
        ),
        out_specs=(
            P(None, "lev", "lat", None, None),
            P(None, "lev", "lat", None, None),
            P("lev", "lat", None),
        ),
        check_vma=False,
    )
```

profile of v0, /device:TPU:0, one launch (start us, length us, event | category | flops | bytes accessed | tf_op | source)
XLA Modules:
  0.0 150.3 jit_solution(6277365626137333626)
XLA Ops:
  7.2 1.0 copy-done.5
  8.3 1.0 copy-done.7
  9.3 0.7 copy-done.24
  10.0 0.1 pack.1
  10.1 0.5 collective-permute-start.3
  10.6 1.2 collective-permute-done.3
  11.9 3.0 %collective-permute-start.4 = (bf16[8,32,512]{2,1,0:T(8,128)(2,1)S(1)}, bf16[8,32,512]{2,1,0:T(8,128)(2,1)S(1)}, u32[]{:S(2)}, u32[]{:S(2)}) collective-permute-start(bf16[8,32,512]{2,1,0:T(8,128)(2,1)S(1)} %add_convert_fusion.1), channel_id=1, source_target_pairs={{0,2},{1,3},{2,0},{3,1},{4,6},{5,7},{6,4},{7,5},{8,10},{9,11},{10,... | collective-permute-start | bytes 786440 | tf_op jit(solution)/shard_map/ppermute | solution.py:399
  14.8 6.6 %collective-permute-done.4 = bf16[8,32,512]{2,1,0:T(8,128)(2,1)S(1)} collective-permute-done((bf16[8,32,512]{2,1,0:T(8,128)(2,1)S(1)}, bf16[8,32,512]{2,1,0:T(8,128)(2,1)S(1)}, u32[]{:S(2)}, u32[]{:S(2)}) %collective-permute-start.4) | collective-permute-done | bytes 262176 | tf_op jit(solution)/shard_map/ppermute | solution.py:399
  21.4 0.8 add_convert_fusion
  22.2 28.2 %all_to_all.25 = bf16[8,32,1024]{2,1,0:T(8,128)(2,1)S(1)} all-to-all(bf16[8,32,1024]{2,1,0:T(8,128)(2,1)S(1)} %get-tuple-element.17), channel_id=1, replica_groups=mesh['lat'=8,'lev'=4] {'lat'}, dimensions={0} | all-to-all | bytes 1048576 | tf_op jit(solution)/shard_map/all_to_all | solution.py:395
  50.4 3.4 %all-to-all-start.2 = ((bf16[8,32,512]{2,1,0:T(8,128)(2,1)}), bf16[8,32,512]{2,1,0:T(8,128)(2,1)S(1)}, u32[]{:S(2)}, u32[]{:S(2)}) async-start(bf16[8,32,512]{2,1,0:T(8,128)(2,1)} %add_convert_fusion), calls=%async_computation.2 | async-start | bytes 524288 | tf_op jit(solution)/shard_map/all_to_all | solution.py:395
  53.9 3.0 %copy-done = bf16[1024,3072]{1,0:T(8,128)(2,1)S(1)} copy-done((bf16[1024,3072]{1,0:T(8,128)(2,1)S(1)}, bf16[1024,3072]{1,0:T(8,128)(2,1)}, u32[]{:S(2)}) %copy-start) | copy-done | bytes 6291480
  56.9 8.3 %forward.1 = (bf16[256,1024]{1,0:T(8,128)(2,1)S(1)}, bf16[256,1024]{1,0:T(8,128)(2,1)S(1)}, bf16[256,1024]{1,0:T(8,128)(2,1)S(1)}, f32[256,1024]{1,0:T(8,128)S(1...) custom-call(bf16[256,1024]{1,0:T(8,128)(2,1)S(1)} %bitcast.17, ...), custom_call_target="tpu_custom_call" | custom-call | flops 3221225472 | bytes 13631488 | tf_op jit(solution)/shard_map/forward/pallas_call | solution.py:208
  65.2 1.3 copy-done.3
  66.6 1.0 copy-done.10
  67.6 1.0 copy-done.12
  68.5 0.8 copy-done.14
  69.3 0.8 copy-done.16
  70.1 0.8 copy-done.18
  70.9 0.8 copy-done.20
  71.7 0.7 copy-done.23
  72.4 5.9 %all-to-all-start.4 = ((bf16[8,256,128]{2,1,0:T(8,128)(2,1)}), bf16[8,256,128]{2,1,0:T(8,128)(2,1)S(1)}, u32[]{:S(2)}, u32[]{:S(2)}) async-start(bf16[8,256,128]{2,1,0:T(8,128)(2,1)} %copy-done.20), calls=%async_computation.4 | async-start | bytes 1048576 | tf_op jit(solution)/shard_map/all_to_all | solution.py:395
  78.4 1.1 add_convert_fusion.3
  79.5 1.6 %collective-permute-start.1 = (bf16[256,512]{1,0:T(8,128)(2,1)S(1)}, bf16[256,512]{1,0:T(8,128)(2,1)S(1)}, u32[]{:S(2)}, u32[]{:S(2)}) collective-permute-start(bf16[256,512]{1,0:T(8,128)(2,1)S(1)} %add_convert_fusion.3), channel_id=1, source_target_pairs={{0,2},{1,3},{2,0},{3,1},{4,6},{5,7},{6,4},{7,5},{8,10},{9,11},{10,... | collective-permute-start | bytes 786440 | tf_op jit(solution)/shard_map/ppermute | solution.py:399
  81.1 6.9 %collective-permute-done.1 = bf16[256,512]{1,0:T(8,128)(2,1)S(1)} collective-permute-done((bf16[256,512]{1,0:T(8,128)(2,1)S(1)}, bf16[256,512]{1,0:T(8,128)(2,1)S(1)}, u32[]{:S(2)}, u32[]{:S(2)}) %collective-permute-start.1) | collective-permute-done | bytes 262176 | tf_op jit(solution)/shard_map/ppermute | solution.py:399
  88.0 0.8 add_convert_fusion.2
  88.7 4.8 %all-to-all-done.4.own_ref = bf16[8,256,128]{2,1,0:T(8,128)(2,1)S(1)} async-done(((bf16[8,256,128]{2,1,0:T(8,128)(2,1)}), bf16[8,256,128]{2,1,0:T(8,128)(2,1)S(1)}, u32[]{:S(2)}, u32[]{:S(2)}) %all-to-all-start.4) | async-done | bytes 524320 | tf_op jit(solution)/shard_map/all_to_all | solution.py:395
  93.5 4.0 %all-to-all-start.1 = ((bf16[8,32,512]{2,1,0:T(8,128)(2,1)}), bf16[8,32,512]{2,1,0:T(8,128)(2,1)}, u32[]{:S(2)}, u32[]{:S(2)}) async-start(bf16[8,32,512]{2,1,0:T(8,128)(2,1)} %bitcast.26), calls=%async_computation.1 | async-start | bytes 524288 | tf_op jit(solution)/shard_map/all_to_all | solution.py:395
  97.6 2.8 %copy-done.1 = bf16[1024,3072]{1,0:T(8,128)(2,1)S(1)} copy-done((bf16[1024,3072]{1,0:T(8,128)(2,1)S(1)}, bf16[1024,3072]{1,0:T(8,128)(2,1)}, u32[]{:S(2)}) %copy-start.1) | copy-done | bytes 6291480
  100.4 1.6 %copy-done.4 = bf16[16,256,256]{2,1,0:T(8,128)(2,1)S(1)} copy-done((bf16[16,256,256]{2,1,0:T(8,128)(2,1)S(1)}, bf16[16,256,256]{2,1,0:T(8,128)(2,1)}, u32[]{:S(2)}) %copy-start.4) | copy-done | bytes 2097176
  102.0 1.2 copy-done.11
  103.2 1.2 copy-done.13
  104.4 1.0 copy-done.15
  105.5 1.0 copy-done.17
  106.5 1.0 copy-done.19
  107.5 14.3 %backward.1 = bf16[256,1024]{1,0:T(8,128)(2,1)} custom-call(bf16[256,1024]{1,0:T(8,128)(2,1)S(1)} %bitcast.18, bf16[256,512]{1,0:T(8,128)(2,1)S(1)} %bitcast.25, bf16[256,512]{1,0:T(8,128)(2,1)} %collective-permute-done.5.other_ref, bf16[1024,1024]{1,0:T(8,128)(2,1)S(1)} %bitcast.16, bf16[1024,3072]{1,0:T(8,128)(2,1)S(1)} %copy-done.1, ...), custom_call_target="tpu_custom_call" | custom-call | flops 4294967296 | bytes 13631488 | tf_op jit(solution)/shard_map/backward/pallas_call | solution.py:321
  121.8 6.0 %all-to-all-start.3 = ((bf16[8,32,1024]{2,1,0:T(8,128)(2,1)}), bf16[8,32,1024]{2,1,0:T(8,128)(2,1)S(1)}, u32[]{:S(2)}, u32[]{:S(2)}) async-start(bf16[8,32,1024]{2,1,0:T(8,128)(2,1)} %bitcast.8), calls=%async_computation.3 | async-start | bytes 1048576 | tf_op jit(solution)/shard_map/all_to_all | solution.py:395
  127.9 0.5 collective-permute-start.2
  128.4 1.4 collective-permute-done.6.other_ref
  129.8 0.8 copy-done.21
  130.6 1.6 %copy-done.9 = bf16[64,32,512]{2,1,0:T(8,128)(2,1)S(1)} copy-done((bf16[64,32,512]{2,1,0:T(8,128)(2,1)S(1)}, bf16[64,32,512]{2,1,0:T(8,128)(2,1)}, u32[]{:S(2)}) %copy-start.9) | copy-done | bytes 2097176
  132.2 1.0 copy-done.22
  133.2 0.7 mix_gradient.1
  133.9 0.2 collective-permute-start.7
  134.1 1.9 %make_output.1 = bf16[2,2,4,16,1024]{4,3,2,1,0:T(8,128)(2,1)} custom-call(bf16[2,2,4,16,1024]{4,3,2,1,0:T(8,128)(2,1)S(1)} %bitcast.20, f32[1,1024]{1,0:T(1,128)S(1)} %copy-done.25, bf16[8,32,512]{2,1,0:T(8,128)(2,1)} %all-to-all-done.1.own_ref, bf16[8,32,512]{2,1,0:T(8,128)(2,1)S(1)} %collective-permute-done.2.other_ref), custom_call_target="tpu_custom_call" | custom-call | tf_op jit(solution)/shard_map/make_output/pallas_call | solution.py:50
  136.1 5.6 %all-to-all-done.3.back_ref = bf16[8,32,1024]{2,1,0:T(8,128)(2,1)S(1)} async-done(((bf16[8,32,1024]{2,1,0:T(8,128)(2,1)}), bf16[8,32,1024]{2,1,0:T(8,128)(2,1)S(1)}, u32[]{:S(2)}, u32[]{:S(2)}) %all-to-all-start.3) | async-done | bytes 524320 | tf_op jit(solution)/shard_map/all_to_all | solution.py:395
  141.7 0.9 make_gradient.1
  142.6 0.8 place.1
  (45 shorter events, 0.2 us)
Async XLA Ops:
  7.2 123.4 %all-gather.3.cloned.1.call-start = ((), (), s32[]{:S(2)}) async-start(), calls=%async_computation.5 | async-start | bytes 2359296 | tf_op jit(solution)/shard_map/all_gather | solution.py:431
  7.2 1.0 copy-start.5
  8.3 1.0 copy-start.7
  9.3 0.7 copy-start.24
  10.0 43.9 %copy-start.2 = (bf16[1,1024,1024]{2,1,0:T(8,128)(2,1)S(1)}, bf16[1,1024,1024]{2,1,0:T(8,128)(2,1)}, u32[]{:S(2)}) copy-start(bf16[1,1024,1024]{2,1,0:T(8,128)(2,1)} %param.9) | copy-start | bytes 6291460
  10.0 43.9 %copy-start.26 = (s32[2,16]{1,0:T(2,128)S(1)}, s32[2,16]{1,0:T(2,128)}, u32[]{:S(2)}) copy-start(s32[2,16]{1,0:T(2,128)} %mask_ref.1) | copy-start | bytes 388
  10.1 1.7 %collective-permute-start.3 = (bf16[8,32,512]{2,1,0:T(8,128)(2,1)S(1)}, bf16[8,32,512]{2,1,0:T(8,128)(2,1)S(1)}, u32[]{:S(2)}, u32[]{:S(2)}) collective-permute-start(bf16[8,32,512]{2,1,0:T(8,128)(2,1)S(1)} %get-tuple-element.21), channel_id=1, source_target_pairs={{0,1},{1,0},{2,3},{3,2},{4,5},{5,4},{6,7},{7,6},{8,9},{9,8},{10,11... | collective-permute-start | bytes 786440 | tf_op jit(solution)/shard_map/ppermute | solution.py:399
  11.9 9.6 %collective-permute-start.4 = (bf16[8,32,512]{2,1,0:T(8,128)(2,1)S(1)}, bf16[8,32,512]{2,1,0:T(8,128)(2,1)S(1)}, u32[]{:S(2)}, u32[]{:S(2)}) collective-permute-start(bf16[8,32,512]{2,1,0:T(8,128)(2,1)S(1)} %add_convert_fusion.1), channel_id=1, source_target_pairs={{0,2},{1,3},{2,0},{3,1},{4,6},{5,7},{6,4},{7,5},{8,10},{9,11},{10,... | collective-permute-start | bytes 786440 | tf_op jit(solution)/shard_map/ppermute | solution.py:399
  50.4 22.0 %all-to-all-start.2 = ((bf16[8,32,512]{2,1,0:T(8,128)(2,1)}), bf16[8,32,512]{2,1,0:T(8,128)(2,1)S(1)}, u32[]{:S(2)}, u32[]{:S(2)}) async-start(bf16[8,32,512]{2,1,0:T(8,128)(2,1)} %add_convert_fusion), calls=%async_computation.2 | async-start | bytes 524288 | tf_op jit(solution)/shard_map/all_to_all | solution.py:395
  53.9 3.1 %copy-start = (bf16[1024,3072]{1,0:T(8,128)(2,1)S(1)}, bf16[1024,3072]{1,0:T(8,128)(2,1)}, u32[]{:S(2)}) copy-start(bf16[1024,3072]{1,0:T(8,128)(2,1)} %wv_ref.3) | copy-start | bytes 18874372
  65.2 1.3 copy-start.3
  66.6 1.0 copy-start.10
  67.6 1.0 copy-start.12
  68.5 0.8 copy-start.14
  69.3 0.8 copy-start.16
  70.1 0.8 copy-start.18
  70.9 0.8 copy-start.20
  71.7 0.7 copy-start.23
  72.4 5.9 %collective-permute-start = (bf16[256,512]{1,0:T(8,128)(2,1)}, bf16[256,512]{1,0:T(8,128)(2,1)}, u32[]{:S(2)}, u32[]{:S(2)}) collective-permute-start(bf16[256,512]{1,0:T(8,128)(2,1)} %get-tuple-element.19), channel_id=1, source_target_pairs={{0,1},{1,0},{2,3},{3,2},{4,5},{5,4},{6,7},{7,6},{8,9},{9,8},{10,11... | collective-permute-start | bytes 786440 | tf_op jit(solution)/shard_map/ppermute | solution.py:399
  72.4 21.1 %all-to-all-start.4 = ((bf16[8,256,128]{2,1,0:T(8,128)(2,1)}), bf16[8,256,128]{2,1,0:T(8,128)(2,1)S(1)}, u32[]{:S(2)}, u32[]{:S(2)}) async-start(bf16[8,256,128]{2,1,0:T(8,128)(2,1)} %copy-done.20), calls=%async_computation.4 | async-start | bytes 1048576 | tf_op jit(solution)/shard_map/all_to_all | solution.py:395
  79.5 8.5 %collective-permute-start.1 = (bf16[256,512]{1,0:T(8,128)(2,1)S(1)}, bf16[256,512]{1,0:T(8,128)(2,1)S(1)}, u32[]{:S(2)}, u32[]{:S(2)}) collective-permute-start(bf16[256,512]{1,0:T(8,128)(2,1)S(1)} %add_convert_fusion.3), channel_id=1, source_target_pairs={{0,2},{1,3},{2,0},{3,1},{4,6},{5,7},{6,4},{7,5},{8,10},{9,11},{10,... | collective-permute-start | bytes 786440 | tf_op jit(solution)/shard_map/ppermute | solution.py:399
  81.0 16.5 %collective-permute-start.5 = (bf16[256,512]{1,0:T(8,128)(2,1)S(1)}, bf16[256,512]{1,0:T(8,128)(2,1)}, u32[]{:S(2)}, u32[]{:S(2)}) collective-permute-start(bf16[256,512]{1,0:T(8,128)(2,1)S(1)} %bitcast.24), channel_id=1, source_target_pairs={{0,1},{1,0},{2,3},{3,2},{4,5},{5,4},{6,7},{7,6},{8,9},{9,8},{10,11... | collective-permute-start | bytes 786440 | tf_op jit(solution)/shard_map/ppermute | solution.py:399
  93.5 28.3 %all-to-all-start.1 = ((bf16[8,32,512]{2,1,0:T(8,128)(2,1)}), bf16[8,32,512]{2,1,0:T(8,128)(2,1)}, u32[]{:S(2)}, u32[]{:S(2)}) async-start(bf16[8,32,512]{2,1,0:T(8,128)(2,1)} %bitcast.26), calls=%async_computation.1 | async-start | bytes 524288 | tf_op jit(solution)/shard_map/all_to_all | solution.py:395
  97.6 2.8 %copy-start.1 = (bf16[1024,3072]{1,0:T(8,128)(2,1)S(1)}, bf16[1024,3072]{1,0:T(8,128)(2,1)}, u32[]{:S(2)}) copy-start(bf16[1024,3072]{1,0:T(8,128)(2,1)} %wv_ref.3) | copy-start | bytes 18874372
  100.4 1.6 %copy-start.4 = (bf16[16,256,256]{2,1,0:T(8,128)(2,1)S(1)}, bf16[16,256,256]{2,1,0:T(8,128)(2,1)}, u32[]{:S(2)}) copy-start(bf16[16,256,256]{2,1,0:T(8,128)(2,1)} %copy-done.3) | copy-start | bytes 6291460
  102.0 1.2 copy-start.11
  103.2 1.2 copy-start.13
  104.4 1.0 copy-start.15
  105.5 1.0 copy-start.17
  106.5 1.0 copy-start.19
  121.8 12.3 %copy-start.6 = (bf16[2,1,2,64,1024]{4,3,2,1,0:T(8,128)(2,1)S(1)}, bf16[2,1,2,64,1024]{4,3,2,1,0:T(8,128)(2,1)}, u32[]{:S(2)}) copy-start(bf16[2,1,2,64,1024]{4,3,2,1,0:T(8,128)(2,1)} %param.6) | copy-start | bytes 1572868
  121.8 12.3 %copy-start.25 = (f32[1,1024]{1,0:T(1,128)S(1)}, f32[1,1024]{1,0:T(1,128)}, u32[]{:S(2)}) copy-start(f32[1,1024]{1,0:T(1,128)} %gain_ref.3) | copy-start | bytes 12292
  121.8 19.9 %all-to-all-start.3 = ((bf16[8,32,1024]{2,1,0:T(8,128)(2,1)}), bf16[8,32,1024]{2,1,0:T(8,128)(2,1)S(1)}, u32[]{:S(2)}, u32[]{:S(2)}) async-start(bf16[8,32,1024]{2,1,0:T(8,128)(2,1)} %bitcast.8), calls=%async_computation.3 | async-start | bytes 1048576 | tf_op jit(solution)/shard_map/all_to_all | solution.py:395
  127.8 1.9 %collective-permute-start.6 = (bf16[8,256,128]{2,1,0:T(8,128)(2,1)S(1)}, bf16[8,256,128]{2,1,0:T(8,128)(2,1)S(1)}, u32[]{:S(2)}, u32[]{:S(2)}) collective-permute-start(bf16[8,256,128]{2,1,0:T(8,128)(2,1)S(1)} %all-to-all-done.4.own_ref), channel_id=1, source_target_pairs={{0,1},{1,0},{2,3},{3,2},{4,5},{5,4},{6,7},{7,6},{8,9},{9,8},{10,11... | collective-permute-start | bytes 1572872 | tf_op jit(solution)/shard_map/ppermute | solution.py:399
  127.9 6.3 %collective-permute-start.2 = (bf16[8,32,512]{2,1,0:T(8,128)(2,1)}, bf16[8,32,512]{2,1,0:T(8,128)(2,1)S(1)}, u32[]{:S(2)}, u32[]{:S(2)}) collective-permute-start(bf16[8,32,512]{2,1,0:T(8,128)(2,1)} %all-to-all-done.1.own_ref), channel_id=1, source_target_pairs={{0,1},{1,0},{2,3},{3,2},{4,5},{5,4},{6,7},{7,6},{8,9},{9,8},{10,11... | collective-permute-start | bytes 786440 | tf_op jit(solution)/shard_map/ppermute | solution.py:399
  129.8 0.8 copy-start.21
  130.6 1.6 %copy-start.9 = (bf16[64,32,512]{2,1,0:T(8,128)(2,1)S(1)}, bf16[64,32,512]{2,1,0:T(8,128)(2,1)}, u32[]{:S(2)}) copy-start(bf16[64,32,512]{2,1,0:T(8,128)(2,1)} %all-gather.3.cloned.1.call-done) | copy-start | bytes 6291460
  132.1 1.0 copy-start.22
  133.2 8.5 %copy-start.8 = (bf16[2,1,2,64,1024]{4,3,2,1,0:T(8,128)(2,1)S(1)}, bf16[2,1,2,64,1024]{4,3,2,1,0:T(8,128)(2,1)}, u32[]{:S(2)}) copy-start(bf16[2,1,2,64,1024]{4,3,2,1,0:T(8,128)(2,1)} %param.11) | copy-start | bytes 1572868
  133.9 8.7 %collective-permute-start.7 = (bf16[128,512]{1,0:T(8,128)(2,1)S(1)}, bf16[128,512]{1,0:T(8,128)(2,1)S(1)}, u32[]{:S(2)}, u32[]{:S(2)}) collective-permute-start(bf16[128,512]{1,0:T(8,128)(2,1)S(1)} %get-tuple-element.30), channel_id=1, source_target_pairs={{0,1},{1,0},{2,3},{3,2},{4,5},{5,4},{6,7},{7,6},{8,9},{9,8},{10,11... | collective-permute-start | bytes 393224 | tf_op jit(solution)/shard_map/ppermute | solution.py:399
Sparse Core Ops, SparseCore 0:
  22.3 57.0 all-gather.2
where the time goes:
time: 151 us; the launch traced here: 150 us
  blocking collectives  28.2 us (19%)
  Pallas kernels  27.1 us (18%)
  waiting for transfers between devices  26.5 us (18%)
  local copies, waits for them, and re-layouts  26.4 us (17%)
  starting transfers between devices  25.2 us (17%)
  between operations  14.2 us (9%)
  other arithmetic  2.69 us (2%)
    all_to_all x1, blocking collectives, swap(): return lax.all_to_all(block, 'lat', split_axis=0, concat_axis=0, tiled=True)  28.2 us
    unnamed x54, local copies, waits for them, and re-layouts  26.4 us
    all_to_all x4, starting transfers between devices, swap(): return lax.all_to_all(block, 'lat', split_axis=0, concat_axis=0, tiled=True)  19.4 us
    ppermute x8, waiting for transfers between devices, from_level(): lax.ppermute(block, 'lev', [(i, i ^ offset) for i in range(lax.axis_size(...  16.1 us
    pallas_call x1, Pallas kernels, backward(): pl.pallas_call(backward_kernel, out_shape=jax.ShapeDtypeStruct((count, wi...  14.3 us
    all_to_all x4, waiting for transfers between devices, swap(): return lax.all_to_all(block, 'lat', split_axis=0, concat_axis=0, tiled=True)  10.4 us
    pallas_call x1, Pallas kernels, forward(): pl.pallas_call(functools.partial(forward_kernel, samples, lat_count, chun...  8.32 us
    ppermute x8, starting transfers between devices, from_level(): lax.ppermute(block, 'lev', [(i, i ^ offset) for i in range(lax.axis_size(...  5.76 us
  transfers between devices with their start and end apart: 13, of which 6 were waited for; matrix products, arithmetic and copies ran while one was open for 1% of the time, Pallas kernels for 17%

commit v1 on v0

--- a/solution.py
+++ b/solution.py
@@ -44,6 +44,10 @@
     half = width // 2
     core = lax.axis_index("lev") % 2
     return pl.ds(pl.multiple_of((core ^ which) * half, half), half)
+
+
+def in_hbm(array):
+    return pltpu.with_memory_space_constraint(array, pltpu.HBM)
 
 
 def call(kernel, name, out_shape, *operands):
@@ -208,9 +212,9 @@
     return pl.pallas_call(
         functools.partial(forward_kernel, samples, lat_count, chunk, owners),
         out_shape=(
-            [jax.ShapeDtypeStruct((count, width), BF16)] * 3
-            + [jax.ShapeDtypeStruct((count, width), F32)] * 2
-            + [jax.ShapeDtypeStruct((HEADS, count, count), BF16)]
+            [pltpu.HBM((count, width), BF16)] * 3
+            + [pltpu.HBM((count, width), F32)] * 2
+            + [pltpu.HBM((HEADS, count, count), BF16)]
             + [jax.ShapeDtypeStruct((owners, count, features), BF16)]
             + [jax.ShapeDtypeStruct((count, width // 2), BF16)] * 2
         ),
@@ -241,7 +245,7 @@
             transcendentals=HEADS * count * count,
         ),
         name="forward",
-    )(tok_col, key_mask, w_qkv, w_qkv, w_qkv, w_mix)
+    )(tok_col, key_mask, *[in_hbm(w_qkv)] * 3, in_hbm(w_mix))
 
 
 def backward_kernel(
@@ -342,17 +346,21 @@
             transcendentals=0,
         ),
         name="backward",
-    )(tok_col, *flow, w_mix, w_qkv, w_qkv, w_qkv, *saved)
-
-
-def mix_gradient_kernel(factor, own_ref, other_ref, flow_ref, own_out, other_out, flow_scr):
-    bands, owners, cells, half = flow_ref.shape
+    )(tok_col, *flow, in_hbm(w_mix), *[in_hbm(w_qkv)] * 3, *map(in_hbm, saved))
+
+
+def mix_gradient_kernel(factor, own_ref, other_ref, *refs):
+    *flow_refs, own_out, other_out, flow_scr = refs
+    bands, owners, cells, share = flow_refs[0].shape
     count = bands * cells
     features = own_ref.shape[-1]
-    for j in range(owners):
-        for p in range(bands):
-            at = j * count + p * cells
-            flow_scr[at : at + cells, :] = flow_ref[p, j]
+    chip = lax.axis_index("lev") // 2
+    for k, ref in enumerate(flow_refs):
+        cols = pl.ds(pl.multiple_of((chip ^ k) * share, share), share)
+        for j in range(owners):
+            for p in range(bands):
+                at = j * count + p * cells
+                flow_scr[at : at + cells, cols] = ref[p, j]
     flow = flow_scr[...]
     own = own_ref[...].reshape(owners * count, features)
     other = other_ref[...].reshape(owners * count, features)
@@ -360,9 +368,9 @@
     other_out[...] = (tn(other, flow) * factor).astype(BF16)
 
 
-def mix_gradient(own, other, flow_all, factor):
+def mix_gradient(own, other, flow_parts, factor):
     owners, count, features = own.shape
-    half = flow_all.shape[-1]
+    half = flow_parts[0].shape[-1] * len(flow_parts)
     return pl.pallas_call(
         functools.partial(mix_gradient_kernel, factor),
         out_shape=[
@@ -377,7 +385,7 @@
             transcendentals=0,
         ),
         name="mix_gradient",
-    )(own, other, flow_all)
+    )(own, other, *flow_parts)
 
 
 def place_kernel(own_ref, other_ref, out_ref):
@@ -399,16 +407,46 @@
     return lax.ppermute(block, "lev", [(i, i ^ offset) for i in range(lax.axis_size("lev"))])
 
 
-def level_total(own, other):
-    total = own
-    received = from_level(other, 1)
-    offset = 1
-    while True:
-        total = (total.astype(F32) + received.astype(F32)).astype(BF16)
+def add_kernel(own_ref, received_ref, *rest):
+    rest[-1][...] = (own_ref[...].astype(F32) + received_ref[...].astype(F32)).astype(BF16)
+
+
+def add(own, received, after=()):
+    whole = pl.BlockSpec(memory_space=pltpu.VMEM)
+    return pl.pallas_call(
+        add_kernel,
+        out_shape=jax.ShapeDtypeStruct(own.shape, BF16),
+        in_specs=[whole, whole] + [pl.BlockSpec(memory_space=pl.ANY)] * len(after),
+        out_specs=whole,
+        compiler_params=params(),
+        name="add",
+    )(own, received, *after)
+
+
+def pair_total(own, other):
+    return add(own, from_level(other, 1))
+
+
+def level_total(total, after):
+    offset = 2
+    while offset < lax.axis_size("lev"):
+        total = add(total, from_level(total, offset), after)
         offset *= 2
-        if offset == lax.axis_size("lev"):
-            return total
-        received = from_level(total, offset)
+    return total
+
+
+def slice_kernel(in_ref, out_ref):
+    share = out_ref.shape[-1]
+    at = pl.multiple_of(lax.axis_index("lev") // 2 * share, share)
+    out_ref[...] = in_ref[:, :, pl.ds(at, share)]
+
+
+def gather_flow(flow_band):
+    chips = lax.axis_size("lev") // 2
+    owners, cells, half = flow_band.shape
+    shape = jax.ShapeDtypeStruct((owners, cells, half // chips), BF16)
+    mine = lax.all_gather(call(slice_kernel, "slice", shape, flow_band), "lat", axis=0)
+    return [mine] + [from_level(mine, 2 * k) for k in range(1, chips)]
 
 
 def on_device(tokens, key_mask, w_qkv, w_mix, level_scale, cotangent):
@@ -425,24 +463,25 @@
 
     tok_send, cot_own, cot_other = pack(tok_band, cot_band, level_scale)
     tok_col = swap(tok_send).reshape(count, width)
-    flow_band = level_total(cot_own, cot_other)
+    flow_band = level_total(pair_total(cot_own, cot_other), (tok_col,))
     flow_own = swap(flow_band).reshape(count, half)
     flow = (flow_own, from_level(flow_own, 1))
-    flow_all = lax.all_gather(flow_band, "lat", axis=0)
+    flow_parts = gather_flow(flow_band)
 
     *saved, attended, mix_own, mix_other = forward(
         tok_col, key_mask, w_qkv, w_mix, chunk, owners
     )
     attended = swap(attended)
-    mix_half = level_total(mix_own, mix_other)
+    mix_pair = pair_total(mix_own, mix_other)
     back_col = backward(tok_col, flow, w_mix, w_qkv, saved)
+    mix_half = level_total(mix_pair, (back_col,))
     back = swap(back_col.reshape(owners, cells, width))
     mix_band = swap(mix_half.reshape(owners, cells, half))
     output = make_output(tok_band, level_scale, (mix_band, from_level(mix_band, 1)))
     d_tokens = make_gradient(cot_band, back)
 
     factor = 1.0 / math.sqrt(count * owners)
-    grad_own, grad_other = mix_gradient(attended, from_level(attended, 1), flow_all, factor)
+    grad_own, grad_other = mix_gradient(attended, from_level(attended, 1), flow_parts, factor)
     mix_grad = place(grad_own, from_level(grad_other, 1))
     return (
         output.reshape(tokens.shape),

time: 151 us -> 117 us (0.77)
  blocking collectives: 28.2 us -> 0 us
  local copies, waits for them, and re-layouts: 26.4 us -> 4.71 us
  waiting for transfers between devices: 26.5 us -> 36.2 us
  Pallas kernels: 27.1 us -> 32 us
  starting transfers between devices: 25.2 us -> 29.3 us
  other arithmetic: 2.69 us -> 0 us
    all_to_all x1 -> x0, blocking collectives: 28.2 us -> none  [swap(): return lax.all_to_all(block, 'lat', split_axis=0, concat_axis=0, tiled=True)]
    unnamed x54 -> x20, local copies, waits for them, and re-layouts: 26.4 us -> 4.71 us
    all_to_all x4 -> x5, waiting for transfers between devices: 10.4 us -> 15.2 us  [swap(): return lax.all_to_all(block, 'lat', split_axis=0, concat_axis=0, tiled=True)]
    ppermute x8 -> x9, waiting for transfers between devices: 16.1 us -> 20.9 us  [from_level(): lax.ppermute(block, 'lev', [(i, i ^ offset) for i in range(lax.axis_size(...]
    all_to_all x4 -> x5, starting transfers between devices: 19.4 us -> 23.4 us  [swap(): return lax.all_to_all(block, 'lat', split_axis=0, concat_axis=0, tiled=True)]
    convert_element_type x4 -> x0, other arithmetic: 2.69 us -> none  [level_total(): total = (total.astype(F32) + received.astype(F32)).astype(BF16)]
    pallas_call x0 -> x4, Pallas kernels: none -> 1.66 us  [add(): pl.pallas_call(add_kernel, out_shape=jax.ShapeDtypeStruct(own.shape, BF16...]
    pallas_call x4 -> x5, Pallas kernels: 3.81 us -> 5.19 us  [call(): pl.pallas_call(kernel, out_shape=out_shape, compiler_params=params(), nam...]
  transfers between devices with their start and end apart: 13 -> 15, of which waited for: 6 -> 9; matrix products, arithmetic and copies ran while one was open for 1% -> 0% of each run, Pallas kernels for 17% -> 24%
where the time goes in v1:
time: 117 us; the launch traced here: 116 us
  waiting for transfers between devices  36.2 us (31%)
  Pallas kernels  32 us (27%)
  starting transfers between devices  29.3 us (25%)
  between operations  14.2 us (12%)
  local copies, waits for them, and re-layouts  4.71 us (4%)
    all_to_all x5, starting transfers between devices, swap(): return lax.all_to_all(block, 'lat', split_axis=0, concat_axis=0, tiled=True)  23.4 us
    ppermute x9, waiting for transfers between devices, from_level(): lax.ppermute(block, 'lev', [(i, i ^ offset) for i in range(lax.axis_size(...  20.9 us
    all_to_all x5, waiting for transfers between devices, swap(): return lax.all_to_all(block, 'lat', split_axis=0, concat_axis=0, tiled=True)  15.2 us
    pallas_call x1, Pallas kernels, backward(): pl.pallas_call(backward_kernel, out_shape=jax.ShapeDtypeStruct((count, wi...  14.5 us
    pallas_call x1, Pallas kernels, forward(): pl.pallas_call(functools.partial(forward_kernel, samples, lat_count, chun...  9.78 us
    ppermute x9, starting transfers between devices, from_level(): lax.ppermute(block, 'lev', [(i, i ^ offset) for i in range(lax.axis_size(...  5.92 us
    pallas_call x5, Pallas kernels, call(): pl.pallas_call(kernel, out_shape=out_shape, compiler_params=params(), nam...  5.19 us
    unnamed x20, local copies, waits for them, and re-layouts  4.71 us
  transfers between devices with their start and end apart: 15, of which 9 were waited for; matrix products, arithmetic and copies ran while one was open for 0% of the time, Pallas kernels for 24%

profile of v1, /device:TPU:0, one launch (start us, length us, event | category | flops | bytes accessed | tf_op | source)
XLA Modules:
  0.0 116.3 jit_solution(4925510882740223352)
XLA Ops:
  7.2 0.0 copy-start
  7.2 1.0 copy-done
  8.2 1.0 copy-done.2
  9.3 0.7 copy-done.7
  9.9 0.9 pack.1
  10.8 7.4 %all-to-all-start = ((bf16[8,32,1024]{2,1,0:T(8,128)(2,1)}), bf16[8,32,1024]{2,1,0:T(8,128)(2,1)S(1)}, u32[]{:S(2)}, u32[]{:S(2)}) async-start(bf16[8,32,1024]{2,1,0:T(8,128)(2,1)} %get-tuple-element.17), calls=%async_computation | async-start | bytes 1048576 | tf_op jit(solution)/shard_map/all_to_all | solution.py:403
  18.2 0.0 all-gather.3.cloned.1.call-start
  18.2 0.1 collective-permute-start.2
  18.3 1.5 %collective-permute-done.2.received_ref = bf16[8,32,512]{2,1,0:T(8,128)(2,1)S(1)} collective-permute-done((bf16[8,32,512]{2,1,0:T(8,128)(2,1)S(1)}, bf16[8,32,512]{2,1,0:T(8,128)(2,1)S(1)}, u32[]{:S(2)}, u32[]{:S(2)}) %collective-permute-start.2) | collective-permute-done | bytes 262176 | tf_op jit(solution)/shard_map/ppermute | solution.py:407
  19.8 0.1 add.5.own_ref
  19.9 1.6 %collective-permute-start.3 = (bf16[8,32,512]{2,1,0:T(8,128)(2,1)S(1)}, bf16[8,32,512]{2,1,0:T(8,128)(2,1)S(1)}, u32[]{:S(2)}, u32[]{:S(2)}) collective-permute-start(bf16[8,32,512]{2,1,0:T(8,128)(2,1)S(1)} %add.5.own_ref), channel_id=1, source_target_pairs={{0,2},{1,3},{2,0},{3,1},{4,6},{5,7},{6,4},{7,5},{8,10},{9,11},{10,... | collective-permute-start | bytes 786440 | tf_op jit(solution)/shard_map/ppermute | solution.py:407
  21.5 6.8 %collective-permute-done.3.received_ref = bf16[8,32,512]{2,1,0:T(8,128)(2,1)S(1)} collective-permute-done((bf16[8,32,512]{2,1,0:T(8,128)(2,1)S(1)}, bf16[8,32,512]{2,1,0:T(8,128)(2,1)S(1)}, u32[]{:S(2)}, u32[]{:S(2)}) %collective-permute-start.3) | collective-permute-done | bytes 262176 | tf_op jit(solution)/shard_map/ppermute | solution.py:407
  28.3 4.4 %all-to-all-done = bf16[8,32,1024]{2,1,0:T(8,128)(2,1)S(1)} async-done(((bf16[8,32,1024]{2,1,0:T(8,128)(2,1)}), bf16[8,32,1024]{2,1,0:T(8,128)(2,1)S(1)}, u32[]{:S(2)}, u32[]{:S(2)}) %all-to-all-start) | async-done | bytes 524320 | tf_op jit(solution)/shard_map/all_to_all | solution.py:403
  32.7 0.8 add.6.in_ref
  33.4 1.6 %slice.1 = bf16[8,32,256]{2,1,0:T(8,128)(2,1)} custom-call(bf16[8,32,512]{2,1,0:T(8,128)(2,1)} %add.6.in_ref), custom_call_target="tpu_custom_call" | custom-call | tf_op jit(solution)/shard_map/slice/pallas_call | solution.py:54
  35.1 0.0 all-gather.3.cloned.1.call-update
  35.1 3.6 %all-to-all-start.1 = ((bf16[8,32,512]{2,1,0:T(8,128)(2,1)}), bf16[8,32,512]{2,1,0:T(8,128)(2,1)S(1)}, u32[]{:S(2)}, u32[]{:S(2)}) async-start(bf16[8,32,512]{2,1,0:T(8,128)(2,1)} %add.6.in_ref), calls=%async_computation.1 | async-start | bytes 524288 | tf_op jit(solution)/shard_map/all_to_all | solution.py:403
  38.7 9.8 %forward.1 = (bf16[256,1024]{1,0:T(8,128)(2,1)}, bf16[256,1024]{1,0:T(8,128)(2,1)}, bf16[256,1024]{1,0:T(8,128)(2,1)}, f32[256,1024]{1,0:T(8,128)}, f32[256,1024...) custom-call(bf16[256,1024]{1,0:T(8,128)(2,1)S(1)} %bitcast.16, ...), custom_call_target="tpu_custom_call" | custom-call | flops 3221225472 | bytes 13631488 | tf_op jit(solution)/shard_map/forward/pallas_call | solution.py:212
  48.5 0.7 all-to-all-done.1
  49.2 5.3 %all-to-all-start.4 = ((bf16[8,256,128]{2,1,0:T(8,128)(2,1)}), bf16[8,256,128]{2,1,0:T(8,128)(2,1)S(1)}, u32[]{:S(2)}, u32[]{:S(2)}) async-start(bf16[8,256,128]{2,1,0:T(8,128)(2,1)} %get-tuple-element.28), calls=%async_computation.4 | async-start | bytes 1048576 | tf_op jit(solution)/shard_map/all_to_all | solution.py:403
  54.5 0.0 collective-permute-start
  54.5 0.5 collective-permute-start.4
  55.0 1.0 collective-permute-done.received_ref
  56.0 0.1 add.4.own_ref
  56.1 1.6 %collective-permute-start.1 = (bf16[256,512]{1,0:T(8,128)(2,1)S(1)}, bf16[256,512]{1,0:T(8,128)(2,1)S(1)}, u32[]{:S(2)}, u32[]{:S(2)}) collective-permute-start(bf16[256,512]{1,0:T(8,128)(2,1)S(1)} %add.4.own_ref), channel_id=1, source_target_pairs={{0,2},{1,3},{2,0},{3,1},{4,6},{5,7},{6,4},{7,5},{8,10},{9,11},{10,... | collective-permute-start | bytes 786440 | tf_op jit(solution)/shard_map/ppermute | solution.py:407
  57.7 0.0 collective-permute-done.4.other_ref
  57.7 14.5 %backward.1.rest_0_ = bf16[256,1024]{1,0:T(8,128)(2,1)} custom-call(bf16[256,1024]{1,0:T(8,128)(2,1)S(1)} %bitcast.17, bf16[256,512]{1,0:T(8,128)(2,1)S(1)} %bitcast.23, bf16[256,512]{1,0:T(8,128)(2,1)S(1)} %collective-permute-done.4.other_ref, bf16[1024,1024]{1,0:T(8,128)(2,1)} %bitcast.27, bf16[1024,3072]{1,0:T(8,128)(2,1)} %wv_ref.3, ...), custom_call_target="tpu_custom_call" | custom-call | flops 4294967296 | bytes 13631488 | tf_op jit(solution)/shard_map/backward/pallas_call | solution.py:325
  72.2 0.0 collective-permute-done.1.received_ref
  72.2 0.8 add.7
  73.0 3.6 %all-to-all-done.4.own_ref = bf16[8,256,128]{2,1,0:T(8,128)(2,1)S(1)} async-done(((bf16[8,256,128]{2,1,0:T(8,128)(2,1)}), bf16[8,256,128]{2,1,0:T(8,128)(2,1)S(1)}, u32[]{:S(2)}, u32[]{:S(2)}) %all-to-all-start.4) | async-done | bytes 524320 | tf_op jit(solution)/shard_map/all_to_all | solution.py:403
  76.6 3.4 %all-to-all-start.2 = ((bf16[8,32,512]{2,1,0:T(8,128)(2,1)}), bf16[8,32,512]{2,1,0:T(8,128)(2,1)S(1)}, u32[]{:S(2)}, u32[]{:S(2)}) async-start(bf16[8,32,512]{2,1,0:T(8,128)(2,1)} %bitcast.5), calls=%async_computation.2 | async-start | bytes 524288 | tf_op jit(solution)/shard_map/all_to_all | solution.py:403
  80.0 0.0 all-gather.3.cloned.1.call-done
  80.1 1.6 %collective-permute-start.7 = (bf16[8,8,32,256]{3,2,1,0:T(8,128)(2,1)}, bf16[8,8,32,256]{3,2,1,0:T(8,128)(2,1)S(1)}, u32[]{:S(2)}, u32[]{:S(2)}) collective-permute-start(bf16[8,8,32,256]{3,2,1,0:T(8,128)(2,1)} %bitcast.24), channel_id=1, source_target_pairs={{0,2},{1,3},{2,0},{3,1},{4,6},{5,7},{6,4},{7,5},{8,10},{9,11},{10,... | collective-permute-start | bytes 3145736 | tf_op jit(solution)/shard_map/ppermute | solution.py:407
  81.7 6.5 %all-to-all-done.2.own_ref = bf16[8,32,512]{2,1,0:T(8,128)(2,1)S(1)} async-done(((bf16[8,32,512]{2,1,0:T(8,128)(2,1)}), bf16[8,32,512]{2,1,0:T(8,128)(2,1)S(1)}, u32[]{:S(2)}, u32[]{:S(2)}) %all-to-all-start.2) | async-done | bytes 262176 | tf_op jit(solution)/shard_map/all_to_all | solution.py:403
  88.2 3.6 %all-to-all-start.3 = ((bf16[8,32,1024]{2,1,0:T(8,128)(2,1)}), bf16[8,32,1024]{2,1,0:T(8,128)(2,1)S(1)}, u32[]{:S(2)}, u32[]{:S(2)}) async-start(bf16[8,32,1024]{2,1,0:T(8,128)(2,1)} %bitcast.8), calls=%async_computation.3 | async-start | bytes 1048576 | tf_op jit(solution)/shard_map/all_to_all | solution.py:403
  91.8 0.0 copy-start.3
  91.8 0.1 collective-permute-start.6
  91.9 0.5 collective-permute-start.5
  92.4 1.4 %collective-permute-done.6.other_ref = bf16[8,256,128]{2,1,0:T(8,128)(2,1)S(1)} collective-permute-done((bf16[8,256,128]{2,1,0:T(8,128)(2,1)S(1)}, bf16[8,256,128]{2,1,0:T(8,128)(2,1)S(1)}, u32[]{:S(2)}, u32[]{:S(2)}) %collective-permute-start.6) | collective-permute-done | bytes 524320 | tf_op jit(solution)/shard_map/ppermute | solution.py:407
  93.8 10.1 %collective-permute-done.7.refs_1_ = bf16[8,8,32,256]{3,2,1,0:T(8,128)(2,1)S(1)} collective-permute-done((bf16[8,8,32,256]{3,2,1,0:T(8,128)(2,1)}, bf16[8,8,32,256]{3,2,1,0:T(8,128)(2,1)S(1)}, u32[]{:S(2)}, u32[]{:S(2)}) %collective-permute-start.7) | collective-permute-done | bytes 1048608 | tf_op jit(solution)/shard_map/ppermute | solution.py:407
  103.9 1.2 %copy-done.4 = bf16[64,32,256]{2,1,0:T(8,128)(2,1)S(1)} copy-done((bf16[64,32,256]{2,1,0:T(8,128)(2,1)S(1)}, bf16[64,32,256]{2,1,0:T(8,128)(2,1)}, u32[]{:S(2)}) %copy-start.4) | copy-done | bytes 1048600
  105.1 0.9 mix_gradient.1
  106.0 0.0 copy-start.5
  106.0 0.7 copy-done.5
  106.7 0.0 collective-permute-start.8
  106.8 1.0 make_output.1
  107.7 0.9 make_gradient.1
  108.7 0.8 place.1
  (15 shorter events, 0.0 us)
Async XLA Ops:
  7.2 1.0 copy-start
  8.2 1.0 copy-start.2
  9.3 0.7 copy-start.7
  10.8 27.9 %copy-start.9 = (s32[2,16]{1,0:T(2,128)S(1)}, s32[2,16]{1,0:T(2,128)}, u32[]{:S(2)}) copy-start(s32[2,16]{1,0:T(2,128)} %mask_ref.1) | copy-start | bytes 388
  10.8 21.9 %all-to-all-start = ((bf16[8,32,1024]{2,1,0:T(8,128)(2,1)}), bf16[8,32,1024]{2,1,0:T(8,128)(2,1)S(1)}, u32[]{:S(2)}, u32[]{:S(2)}) async-start(bf16[8,32,1024]{2,1,0:T(8,128)(2,1)} %get-tuple-element.17), calls=%async_computation | async-start | bytes 1048576 | tf_op jit(solution)/shard_map/all_to_all | solution.py:403
  18.2 61.9 %all-gather.3.cloned.1.call-start = ((), (), s32[]{:S(2)}) async-start(), calls=%async_computation.5 | async-start | bytes 1179648 | tf_op jit(solution)/shard_map/all_gather | solution.py:448
  18.2 1.6 %collective-permute-start.2 = (bf16[8,32,512]{2,1,0:T(8,128)(2,1)S(1)}, bf16[8,32,512]{2,1,0:T(8,128)(2,1)S(1)}, u32[]{:S(2)}, u32[]{:S(2)}) collective-permute-start(bf16[8,32,512]{2,1,0:T(8,128)(2,1)S(1)} %get-tuple-element.21), channel_id=1, source_target_pairs={{0,1},{1,0},{2,3},{3,2},{4,5},{5,4},{6,7},{7,6},{8,9},{9,8},{10,11... | collective-permute-start | bytes 786440 | tf_op jit(solution)/shard_map/ppermute | solution.py:407
  19.9 8.4 %collective-permute-start.3 = (bf16[8,32,512]{2,1,0:T(8,128)(2,1)S(1)}, bf16[8,32,512]{2,1,0:T(8,128)(2,1)S(1)}, u32[]{:S(2)}, u32[]{:S(2)}) collective-permute-start(bf16[8,32,512]{2,1,0:T(8,128)(2,1)S(1)} %add.5.own_ref), channel_id=1, source_target_pairs={{0,2},{1,3},{2,0},{3,1},{4,6},{5,7},{6,4},{7,5},{8,10},{9,11},{10,... | collective-permute-start | bytes 786440 | tf_op jit(solution)/shard_map/ppermute | solution.py:407
  35.1 14.1 %all-to-all-start.1 = ((bf16[8,32,512]{2,1,0:T(8,128)(2,1)}), bf16[8,32,512]{2,1,0:T(8,128)(2,1)S(1)}, u32[]{:S(2)}, u32[]{:S(2)}) async-start(bf16[8,32,512]{2,1,0:T(8,128)(2,1)} %add.6.in_ref), calls=%async_computation.1 | async-start | bytes 524288 | tf_op jit(solution)/shard_map/all_to_all | solution.py:403
  49.2 27.4 %all-to-all-start.4 = ((bf16[8,256,128]{2,1,0:T(8,128)(2,1)}), bf16[8,256,128]{2,1,0:T(8,128)(2,1)S(1)}, u32[]{:S(2)}, u32[]{:S(2)}) async-start(bf16[8,256,128]{2,1,0:T(8,128)(2,1)} %get-tuple-element.28), calls=%async_computation.4 | async-start | bytes 1048576 | tf_op jit(solution)/shard_map/all_to_all | solution.py:403
  54.5 1.5 %collective-permute-start = (bf16[256,512]{1,0:T(8,128)(2,1)S(1)}, bf16[256,512]{1,0:T(8,128)(2,1)S(1)}, u32[]{:S(2)}, u32[]{:S(2)}) collective-permute-start(bf16[256,512]{1,0:T(8,128)(2,1)S(1)} %get-tuple-element.19), channel_id=1, source_target_pairs={{0,1},{1,0},{2,3},{3,2},{4,5},{5,4},{6,7},{7,6},{8,9},{9,8},{10,11... | collective-permute-start | bytes 786440 | tf_op jit(solution)/shard_map/ppermute | solution.py:407
  54.5 3.2 %collective-permute-start.4 = (bf16[256,512]{1,0:T(8,128)(2,1)S(1)}, bf16[256,512]{1,0:T(8,128)(2,1)S(1)}, u32[]{:S(2)}, u32[]{:S(2)}) collective-permute-start(bf16[256,512]{1,0:T(8,128)(2,1)S(1)} %bitcast.22), channel_id=1, source_target_pairs={{0,1},{1,0},{2,3},{3,2},{4,5},{5,4},{6,7},{7,6},{8,9},{9,8},{10,11... | collective-permute-start | bytes 786440 | tf_op jit(solution)/shard_map/ppermute | solution.py:407
  56.1 16.1 %collective-permute-start.1 = (bf16[256,512]{1,0:T(8,128)(2,1)S(1)}, bf16[256,512]{1,0:T(8,128)(2,1)S(1)}, u32[]{:S(2)}, u32[]{:S(2)}) collective-permute-start(bf16[256,512]{1,0:T(8,128)(2,1)S(1)} %add.4.own_ref), channel_id=1, source_target_pairs={{0,2},{1,3},{2,0},{3,1},{4,6},{5,7},{6,4},{7,5},{8,10},{9,11},{10,... | collective-permute-start | bytes 786440 | tf_op jit(solution)/shard_map/ppermute | solution.py:407
  76.6 11.6 %all-to-all-start.2 = ((bf16[8,32,512]{2,1,0:T(8,128)(2,1)}), bf16[8,32,512]{2,1,0:T(8,128)(2,1)S(1)}, u32[]{:S(2)}, u32[]{:S(2)}) async-start(bf16[8,32,512]{2,1,0:T(8,128)(2,1)} %bitcast.5), calls=%async_computation.2 | async-start | bytes 524288 | tf_op jit(solution)/shard_map/all_to_all | solution.py:403
  80.1 23.9 %collective-permute-start.7 = (bf16[8,8,32,256]{3,2,1,0:T(8,128)(2,1)}, bf16[8,8,32,256]{3,2,1,0:T(8,128)(2,1)S(1)}, u32[]{:S(2)}, u32[]{:S(2)}) collective-permute-start(bf16[8,8,32,256]{3,2,1,0:T(8,128)(2,1)} %bitcast.24), channel_id=1, source_target_pairs={{0,2},{1,3},{2,0},{3,1},{4,6},{5,7},{6,4},{7,5},{8,10},{9,11},{10,... | collective-permute-start | bytes 3145736 | tf_op jit(solution)/shard_map/ppermute | solution.py:407
  88.2 18.5 %copy-start.1 = (bf16[2,1,2,64,1024]{4,3,2,1,0:T(8,128)(2,1)S(1)}, bf16[2,1,2,64,1024]{4,3,2,1,0:T(8,128)(2,1)}, u32[]{:S(2)}) copy-start(bf16[2,1,2,64,1024]{4,3,2,1,0:T(8,128)(2,1)} %param.6) | copy-start | bytes 1572868
  88.2 18.5 %copy-start.8 = (f32[1,1024]{1,0:T(1,128)S(1)}, f32[1,1024]{1,0:T(1,128)}, u32[]{:S(2)}) copy-start(f32[1,1024]{1,0:T(1,128)} %gain_ref.3) | copy-start | bytes 12292
  88.2 19.5 %all-to-all-start.3 = ((bf16[8,32,1024]{2,1,0:T(8,128)(2,1)}), bf16[8,32,1024]{2,1,0:T(8,128)(2,1)S(1)}, u32[]{:S(2)}, u32[]{:S(2)}) async-start(bf16[8,32,1024]{2,1,0:T(8,128)(2,1)} %bitcast.8), calls=%async_computation.3 | async-start | bytes 1048576 | tf_op jit(solution)/shard_map/all_to_all | solution.py:403
  91.8 15.9 %copy-start.3 = (bf16[2,1,2,64,1024]{4,3,2,1,0:T(8,128)(2,1)S(1)}, bf16[2,1,2,64,1024]{4,3,2,1,0:T(8,128)(2,1)}, u32[]{:S(2)}) copy-start(bf16[2,1,2,64,1024]{4,3,2,1,0:T(8,128)(2,1)} %param.11) | copy-start | bytes 1572868
  91.8 2.0 %collective-permute-start.6 = (bf16[8,256,128]{2,1,0:T(8,128)(2,1)S(1)}, bf16[8,256,128]{2,1,0:T(8,128)(2,1)S(1)}, u32[]{:S(2)}, u32[]{:S(2)}) collective-permute-start(bf16[8,256,128]{2,1,0:T(8,128)(2,1)S(1)} %all-to-all-done.4.own_ref), channel_id=1, source_target_pairs={{0,1},{1,0},{2,3},{3,2},{4,5},{5,4},{6,7},{7,6},{8,9},{9,8},{10,11... | collective-permute-start | bytes 1572872 | tf_op jit(solution)/shard_map/ppermute | solution.py:407
  91.9 14.8 %collective-permute-start.5 = (bf16[8,32,512]{2,1,0:T(8,128)(2,1)S(1)}, bf16[8,32,512]{2,1,0:T(8,128)(2,1)S(1)}, u32[]{:S(2)}, u32[]{:S(2)}) collective-permute-start(bf16[8,32,512]{2,1,0:T(8,128)(2,1)S(1)} %all-to-all-done.2.own_ref), channel_id=1, source_target_pairs={{0,1},{1,0},{2,3},{3,2},{4,5},{5,4},{6,7},{7,6},{8,9},{9,8},{10,11... | collective-permute-start | bytes 786440 | tf_op jit(solution)/shard_map/ppermute | solution.py:407
  103.9 1.2 %copy-start.4 = (bf16[64,32,256]{2,1,0:T(8,128)(2,1)S(1)}, bf16[64,32,256]{2,1,0:T(8,128)(2,1)}, u32[]{:S(2)}) copy-start(bf16[64,32,256]{2,1,0:T(8,128)(2,1)} %all-gather.3.cloned.1.call-done) | copy-start | bytes 3145732
  106.0 0.7 copy-start.5
  106.7 1.9 %copy-start.6 = (f32[128,512]{1,0:T(8,128)S(1)}, f32[128,512]{1,0:T(8,128)}, u32[]{:S(2)}) copy-start(f32[128,512]{1,0:T(8,128)} %copy-done.5) | copy-start | bytes 786436
  106.7 1.9 %collective-permute-start.8 = (bf16[128,512]{1,0:T(8,128)(2,1)S(1)}, bf16[128,512]{1,0:T(8,128)(2,1)S(1)}, u32[]{:S(2)}, u32[]{:S(2)}) collective-permute-start(bf16[128,512]{1,0:T(8,128)(2,1)S(1)} %get-tuple-element.30), channel_id=1, source_target_pairs={{0,1},{1,0},{2,3},{3,2},{4,5},{5,4},{6,7},{7,6},{8,9},{9,8},{10,11... | collective-permute-start | bytes 393224 | tf_op jit(solution)/shard_map/ppermute | solution.py:407
Sparse Core Ops, SparseCore 0:
  35.2 42.1 all-gather.2

commit v2 on v1

--- a/solution.py
+++ b/solution.py
@@ -82,9 +82,9 @@
         "pack",
         [jax.ShapeDtypeStruct(shape + (width,), BF16)]
         + [jax.ShapeDtypeStruct(shape + (width // 2,), BF16)] * 2,
-        tokens,
-        cot,
-        gain,
+        in_hbm(tokens),
+        in_hbm(cot),
+        in_hbm(gain),
     )
 
 
@@ -93,13 +93,14 @@
     for s, ref in enumerate((own_ref, other_ref)):
         cols = half_cols(s, width)
         gain = gain_ref[:, cols]
-        for b in range(batch):
-            for q in range(parts):
-                for r in range(rows):
-                    mixed = ref[b * parts + q, r * chunk : (r + 1) * chunk, :].astype(F32)
-                    out_ref[b, r, q, :, cols] = (
-                        tok_ref[b, r, q, :, cols].astype(F32) + gain * mixed
-                    ).astype(BF16)
+        for t in range(batch * parts):
+            owner = lax.axis_index("lat") ^ t
+            b, q = owner // parts, owner % parts
+            for r in range(rows):
+                mixed = ref[t, r * chunk : (r + 1) * chunk, :].astype(F32)
+                out_ref[b, r, q, :, cols] = (
+                    tok_ref[b, r, q, :, cols].astype(F32) + gain * mixed
+                ).astype(BF16)
 
 
 def make_output(tokens, gain, mixed):
@@ -170,8 +171,8 @@
     qn_ref[...] = qn
     kn_ref[...] = kn
     v_ref[...] = v
-    rq_ref[...] = rq
-    rk_ref[...] = rk
+    rq_ref[...] = rq.astype(BF16)
+    rk_ref[...] = rk.astype(BF16)
     keep = keep_ref[...]
     lane = lax.broadcasted_iota(jnp.int32, (count, 128), 1) // head_width
     per_tile = 128 // head_width
@@ -212,8 +213,7 @@
     return pl.pallas_call(
         functools.partial(forward_kernel, samples, lat_count, chunk, owners),
         out_shape=(
-            [pltpu.HBM((count, width), BF16)] * 3
-            + [pltpu.HBM((count, width), F32)] * 2
+            [pltpu.HBM((count, width), BF16)] * 5
             + [pltpu.HBM((HEADS, count, count), BF16)]
             + [jax.ShapeDtypeStruct((owners, count, features), BF16)]
             + [jax.ShapeDtypeStruct((count, width // 2), BF16)] * 2
@@ -292,7 +292,7 @@
     def through_norm(upstream, unit, factor):
         unit = unit.astype(F32)
         inner = nn((upstream * unit).astype(BF16), mean_mat)
-        return (factor * (upstream - unit * inner)).astype(BF16)
+        return (factor.astype(F32) * (upstream - unit * inner)).astype(BF16)
 
     gq = through_norm(dq, qn, rq_ref[...])
     gk = through_norm(dk, kn, rk_ref[...])
@@ -354,9 +354,8 @@
     bands, owners, cells, share = flow_refs[0].shape
     count = bands * cells
     features = own_ref.shape[-1]
-    chip = lax.axis_index("lev") // 2
     for k, ref in enumerate(flow_refs):
-        cols = pl.ds(pl.multiple_of((chip ^ k) * share, share), share)
+        cols = slice(k * share, (k + 1) * share)
         for j in range(owners):
             for p in range(bands):
                 at = j * count + p * cells
@@ -407,46 +406,82 @@
     return lax.ppermute(block, "lev", [(i, i ^ offset) for i in range(lax.axis_size("lev"))])
 
 
-def add_kernel(own_ref, received_ref, *rest):
-    rest[-1][...] = (own_ref[...].astype(F32) + received_ref[...].astype(F32)).astype(BF16)
-
-
-def add(own, received, after=()):
+def add_kernel(own_ref, received_ref, out_ref):
+    out_ref[...] = (own_ref[...].astype(F32) + received_ref[...].astype(F32)).astype(BF16)
+
+
+def add(own, received):
+    return call(add_kernel, "add", jax.ShapeDtypeStruct(own.shape, BF16), own, received)
+
+
+def pair_total(own, other):
+    return add(own, from_level(other, 1))
+
+
+def before_last(total):
+    offset = 2
+    while 2 * offset < lax.axis_size("lev"):
+        total = add(total, from_level(total, offset))
+        offset *= 2
+    return total, from_level(total, offset)
+
+
+def add_flow_kernel(own_ref, received_ref, _, out_ref, *part_refs):
+    total = (own_ref[...].astype(F32) + received_ref[...].astype(F32)).astype(BF16)
+    out_ref[...] = total
+    share = part_refs[0].shape[-1]
+    for k, ref in enumerate(part_refs):
+        ref[...] = total[:, :, k * share : (k + 1) * share]
+
+
+def add_flow(own, received, after):
+    owners, cells, half = own.shape
+    whole = pl.BlockSpec(memory_space=pltpu.VMEM)
+    part = jax.ShapeDtypeStruct((owners, cells, half // 2), BF16)
+    return pl.pallas_call(
+        add_flow_kernel,
+        out_shape=[jax.ShapeDtypeStruct(own.shape, BF16), part, part],
+        in_specs=[whole, whole, pl.BlockSpec(memory_space=pl.ANY)],
+        out_specs=[whole] * 3,
+        compiler_params=params(),
+        name="add_flow",
+    )(own, received, after)
+
+
+def add_mixed_kernel(own_ref, received_ref, _, *out_refs):
+    for t, out_ref in enumerate(out_refs):
+        band = lax.axis_index("lat") ^ t
+        out_ref[...] = (own_ref[band].astype(F32) + received_ref[band].astype(F32)).astype(BF16)
+
+
+def add_mixed(own, received, after):
+    owners, cells, half = own.shape
     whole = pl.BlockSpec(memory_space=pltpu.VMEM)
     return pl.pallas_call(
-        add_kernel,
-        out_shape=jax.ShapeDtypeStruct(own.shape, BF16),
-        in_specs=[whole, whole] + [pl.BlockSpec(memory_space=pl.ANY)] * len(after),
-        out_specs=whole,
+        add_mixed_kernel,
+        out_shape=[jax.ShapeDtypeStruct((cells, half), BF16)] * owners,
+        in_specs=[whole, whole, pl.BlockSpec(memory_space=pl.ANY)],
+        out_specs=[whole] * owners,
         compiler_params=params(),
-        name="add",
-    )(own, received, *after)
-
-
-def pair_total(own, other):
-    return add(own, from_level(other, 1))
-
-
-def level_total(total, after):
-    offset = 2
-    while offset < lax.axis_size("lev"):
-        total = add(total, from_level(total, offset), after)
-        offset *= 2
-    return total
-
-
-def slice_kernel(in_ref, out_ref):
-    share = out_ref.shape[-1]
-    at = pl.multiple_of(lax.axis_index("lev") // 2 * share, share)
-    out_ref[...] = in_ref[:, :, pl.ds(at, share)]
-
-
-def gather_flow(flow_band):
-    chips = lax.axis_size("lev") // 2
-    owners, cells, half = flow_band.shape
-    shape = jax.ShapeDtypeStruct((owners, cells, half // chips), BF16)
-    mine = lax.all_gather(call(slice_kernel, "slice", shape, flow_band), "lat", axis=0)
-    return [mine] + [from_level(mine, 2 * k) for k in range(1, chips)]
+        name="add_mixed",
+    )(own, received, after)
+
+
+def join_kernel(*refs):
+    for t, ref in enumerate(refs[:-1]):
+        refs[-1][t] = ref[...]
+
+
+def to_bands(parts):
+    owners = len(parts)
+    cells, half = parts[0].shape
+    received = [parts[0]] + [
+        lax.ppermute(parts[t], "lat", [(i, i ^ t) for i in range(owners)])
+        for t in range(1, owners)
+    ]
+    return call(
+        join_kernel, "join", jax.ShapeDtypeStruct((owners, cells, half), BF16), *received
+    )
 
 
 def on_device(tokens, key_mask, w_qkv, w_mix, level_scale, cotangent):
@@ -463,20 +498,20 @@
 
     tok_send, cot_own, cot_other = pack(tok_band, cot_band, level_scale)
     tok_col = swap(tok_send).reshape(count, width)
-    flow_band = level_total(pair_total(cot_own, cot_other), (tok_col,))
+    flow_band, *flow_parts = add_flow(*before_last(pair_total(cot_own, cot_other)), tok_col)
     flow_own = swap(flow_band).reshape(count, half)
     flow = (flow_own, from_level(flow_own, 1))
-    flow_parts = gather_flow(flow_band)
+    flow_parts = [lax.all_gather(part, "lat", axis=0) for part in flow_parts]
 
     *saved, attended, mix_own, mix_other = forward(
         tok_col, key_mask, w_qkv, w_mix, chunk, owners
     )
     attended = swap(attended)
-    mix_pair = pair_total(mix_own, mix_other)
+    mix_terms = before_last(pair_total(mix_own, mix_other))
     back_col = backward(tok_col, flow, w_mix, w_qkv, saved)
-    mix_half = level_total(mix_pair, (back_col,))
     back = swap(back_col.reshape(owners, cells, width))
-    mix_band = swap(mix_half.reshape(owners, cells, half))
+    mix_terms = [term.reshape(owners, cells, half) for term in mix_terms]
+    mix_band = to_bands(add_mixed(*mix_terms, back_col))
     output = make_output(tok_band, level_scale, (mix_band, from_level(mix_band, 1)))
     d_tokens = make_gradient(cot_band, back)
 

time: 117 us -> 132 us (1.13)
  waiting for transfers between devices: 36.2 us -> 48 us
  starting transfers between devices: 29.3 us -> 35.9 us
  local copies, waits for them, and re-layouts: 4.71 us -> 2.47 us
  Pallas kernels: 32 us -> 30.6 us
    all_gather x1 -> x2, waiting for transfers between devices: 0.02 us -> 12.1 us  [on_device(): flow_parts = [lax.all_gather(part, 'lat', axis=0) for part in flow_parts]]
    ppermute x0 -> x7, starting transfers between devices: none -> 11.5 us  [to_bands(): lax.ppermute(parts[t], 'lat', [(i, i ^ t) for i in range(owners)])]
    ppermute x0 -> x7, waiting for transfers between devices: none -> 6.33 us  [to_bands(): lax.ppermute(parts[t], 'lat', [(i, i ^ t) for i in range(owners)])]
    all_to_all x5 -> x4, waiting for transfers between devices: 15.2 us -> 11.1 us  [swap(): return lax.all_to_all(block, 'lat', split_axis=0, concat_axis=0, tiled=True)]
    ppermute x9 -> x8, waiting for transfers between devices: 20.9 us -> 17.7 us  [from_level(): lax.ppermute(block, 'lev', [(i, i ^ offset) for i in range(lax.axis_size(...]
    all_to_all x5 -> x4, starting transfers between devices: 23.4 us -> 20.4 us  [swap(): return lax.all_to_all(block, 'lat', split_axis=0, concat_axis=0, tiled=True)]
    unnamed x20 -> x12, local copies, waits for them, and re-layouts: 4.71 us -> 2.47 us
    ppermute x9 -> x8, starting transfers between devices: 5.92 us -> 3.95 us  [from_level(): lax.ppermute(block, 'lev', [(i, i ^ offset) for i in range(lax.axis_size(...]
  transfers between devices with their start and end apart: 15 -> 21, of which waited for: 9 -> 12; matrix products, arithmetic and copies ran while one was open for 0% -> 0% of each run, Pallas kernels for 24% -> 20%
where the time goes in v2:
time: 132 us; the launch traced here: 131 us
  waiting for transfers between devices  48 us (36%)
  starting transfers between devices  35.9 us (27%)
  Pallas kernels  30.6 us (23%)
  between operations  14.2 us (11%)
  local copies, waits for them, and re-layouts  2.47 us (2%)
    all_to_all x4, starting transfers between devices, swap(): return lax.all_to_all(block, 'lat', split_axis=0, concat_axis=0, tiled=True)  20.4 us
    ppermute x8, waiting for transfers between devices, from_level(): lax.ppermute(block, 'lev', [(i, i ^ offset) for i in range(lax.axis_size(...  17.7 us
    pallas_call x1, Pallas kernels, backward(): pl.pallas_call(backward_kernel, out_shape=jax.ShapeDtypeStruct((count, wi...  14.4 us
    all_gather x2, waiting for transfers between devices, on_device(): flow_parts = [lax.all_gather(part, 'lat', axis=0) for part in flow_parts]  12.1 us
    ppermute x7, starting transfers between devices, to_bands(): lax.ppermute(parts[t], 'lat', [(i, i ^ t) for i in range(owners)])  11.5 us
    all_to_all x4, waiting for transfers between devices, swap(): return lax.all_to_all(block, 'lat', split_axis=0, concat_axis=0, tiled=True)  11.1 us
    pallas_call x1, Pallas kernels, forward(): pl.pallas_call(functools.partial(forward_kernel, samples, lat_count, chun...  9.58 us
    ppermute x7, waiting for transfers between devices, to_bands(): lax.ppermute(parts[t], 'lat', [(i, i ^ t) for i in range(owners)])  6.33 us
  transfers between devices with their start and end apart: 21, of which 12 were waited for; matrix products, arithmetic and copies ran while one was open for 0% of the time, Pallas kernels for 20%

profile of v2, /device:TPU:0, one launch (start us, length us, event | category | flops | bytes accessed | tf_op | source)
XLA Modules:
  0.0 131.1 jit_solution(2680967054570986123)
XLA Ops:
  7.2 2.1 %pack.1 = (bf16[8,32,1024]{2,1,0:T(8,128)(2,1)}, bf16[8,32,512]{2,1,0:T(8,128)(2,1)S(1)}, bf16[8,32,512]{2,1,0:T(8,128)(2,1)S(1)}) custom-call(bf16[2,2,4,16,1024]{4,3,2,1,0:T(8,128)(2,1)} %bitcast.20, bf16[2,2,4,16,1024]{4,3,2,1,0:T(8,128)(2,1)} %bitcast.22, f32[1,1024]{1,0:T(1,128)} %gain_ref.3), custom_call_target="tpu_custom_call" | custom-call | tf_op jit(solution)/shard_map/pack/pallas_call | solution.py:54
  9.2 7.4 %all-to-all-start = ((bf16[8,32,1024]{2,1,0:T(8,128)(2,1)}), bf16[8,32,1024]{2,1,0:T(8,128)(2,1)S(1)}, u32[]{:S(2)}, u32[]{:S(2)}) async-start(bf16[8,32,1024]{2,1,0:T(8,128)(2,1)} %get-tuple-element.28), calls=%async_computation | async-start | bytes 1048576 | tf_op jit(solution)/shard_map/all_to_all | solution.py:402
  16.6 0.0 all-gather.5.cloned.1.call-start
  16.6 0.1 collective-permute-start.2
  16.7 1.5 %collective-permute-done.2.received_ref = bf16[8,32,512]{2,1,0:T(8,128)(2,1)S(1)} collective-permute-done((bf16[8,32,512]{2,1,0:T(8,128)(2,1)S(1)}, bf16[8,32,512]{2,1,0:T(8,128)(2,1)S(1)}, u32[]{:S(2)}, u32[]{:S(2)}) %collective-permute-start.2) | collective-permute-done | bytes 262176 | tf_op jit(solution)/shard_map/ppermute | solution.py:406
  18.2 0.1 add.3.own_ref
  18.3 1.6 %collective-permute-start.3 = (bf16[8,32,512]{2,1,0:T(8,128)(2,1)S(1)}, bf16[8,32,512]{2,1,0:T(8,128)(2,1)S(1)}, u32[]{:S(2)}, u32[]{:S(2)}) collective-permute-start(bf16[8,32,512]{2,1,0:T(8,128)(2,1)S(1)} %add.3.own_ref), channel_id=1, source_target_pairs={{0,2},{1,3},{2,0},{3,1},{4,6},{5,7},{6,4},{7,5},{8,10},{9,11},{10,... | collective-permute-start | bytes 786440 | tf_op jit(solution)/shard_map/ppermute | solution.py:406
  19.9 6.8 %collective-permute-done.3.received_ref = bf16[8,32,512]{2,1,0:T(8,128)(2,1)S(1)} collective-permute-done((bf16[8,32,512]{2,1,0:T(8,128)(2,1)S(1)}, bf16[8,32,512]{2,1,0:T(8,128)(2,1)S(1)}, u32[]{:S(2)}, u32[]{:S(2)}) %collective-permute-start.3) | collective-permute-done | bytes 262176 | tf_op jit(solution)/shard_map/ppermute | solution.py:406
  26.7 4.4 %all-to-all-done = bf16[8,32,1024]{2,1,0:T(8,128)(2,1)S(1)} async-done(((bf16[8,32,1024]{2,1,0:T(8,128)(2,1)}), bf16[8,32,1024]{2,1,0:T(8,128)(2,1)S(1)}, u32[]{:S(2)}, u32[]{:S(2)}) %all-to-all-start) | async-done | bytes 524320 | tf_op jit(solution)/shard_map/all_to_all | solution.py:402
  31.1 0.8 add_flow.1
  31.9 0.0 all-gather.5.cloned.1.call-update
  31.9 3.6 %all-to-all-start.1 = ((bf16[8,32,512]{2,1,0:T(8,128)(2,1)}), bf16[8,32,512]{2,1,0:T(8,128)(2,1)S(1)}, u32[]{:S(2)}, u32[]{:S(2)}) async-start(bf16[8,32,512]{2,1,0:T(8,128)(2,1)} %get-tuple-element.33), calls=%async_computation.1 | async-start | bytes 524288 | tf_op jit(solution)/shard_map/all_to_all | solution.py:402
  35.6 0.0 all-gather.7.cloned.1.call-start
  35.6 0.7 all-gather.7.cloned.1.call-update
  36.4 9.6 %forward.1 = (bf16[256,1024]{1,0:T(8,128)(2,1)}, bf16[256,1024]{1,0:T(8,128)(2,1)}, bf16[256,1024]{1,0:T(8,128)(2,1)}, bf16[256,1024]{1,0:T(8,128)(2,1)}, bf16[2...) custom-call(bf16[256,1024]{1,0:T(8,128)(2,1)S(1)} %bitcast.18, ...), custom_call_target="tpu_custom_call" | custom-call | flops 3221225472 | bytes 13631488 | tf_op jit(solution)/shard_map/forward/pallas_call | solution.py:213
  45.9 0.1 all-to-all-done.1
  46.1 5.9 %all-to-all-start.3 = ((bf16[8,256,128]{2,1,0:T(8,128)(2,1)}), bf16[8,256,128]{2,1,0:T(8,128)(2,1)S(1)}, u32[]{:S(2)}, u32[]{:S(2)}) async-start(bf16[8,256,128]{2,1,0:T(8,128)(2,1)} %get-tuple-element.48), calls=%async_computation.3 | async-start | bytes 1048576 | tf_op jit(solution)/shard_map/all_to_all | solution.py:402
  52.0 1.5 %collective-permute-done.4.other_ref = bf16[256,512]{1,0:T(8,128)(2,1)S(1)} collective-permute-done((bf16[256,512]{1,0:T(8,128)(2,1)S(1)}, bf16[256,512]{1,0:T(8,128)(2,1)S(1)}, u32[]{:S(2)}, u32[]{:S(2)}) %collective-permute-start.4) | collective-permute-done | bytes 262176 | tf_op jit(solution)/shard_map/ppermute | solution.py:406
  53.5 14.4 %backward.1._ = bf16[256,1024]{1,0:T(8,128)(2,1)} custom-call(bf16[256,1024]{1,0:T(8,128)(2,1)S(1)} %bitcast.19, bf16[256,512]{1,0:T(8,128)(2,1)S(1)} %bitcast.28, bf16[256,512]{1,0:T(8,128)(2,1)S(1)} %collective-permute-done.4.other_ref, bf16[1024,1024]{1,0:T(8,128)(2,1)} %bitcast.31, bf16[1024,3072]{1,0:T(8,128)(2,1)} %wv_ref.3, ...), custom_call_target="tpu_custom_call" | custom-call | flops 4294967296 | bytes 13631488 | tf_op jit(solution)/shard_map/backward/pallas_call | solution.py:325
  67.9 6.6 %all-to-all-done.3.own_ref = bf16[8,256,128]{2,1,0:T(8,128)(2,1)S(1)} async-done(((bf16[8,256,128]{2,1,0:T(8,128)(2,1)}), bf16[8,256,128]{2,1,0:T(8,128)(2,1)S(1)}, u32[]{:S(2)}, u32[]{:S(2)}) %all-to-all-start.3) | async-done | bytes 524320 | tf_op jit(solution)/shard_map/all_to_all | solution.py:402
  74.5 3.5 %all-to-all-start.2 = ((bf16[8,32,1024]{2,1,0:T(8,128)(2,1)}), bf16[8,32,1024]{2,1,0:T(8,128)(2,1)S(1)}, u32[]{:S(2)}, u32[]{:S(2)}) async-start(bf16[8,32,1024]{2,1,0:T(8,128)(2,1)} %bitcast.9), calls=%async_computation.2 | async-start | bytes 1048576 | tf_op jit(solution)/shard_map/all_to_all | solution.py:402
  78.0 0.1 collective-permute-start
  78.1 0.5 collective-permute-start.13
  78.6 1.0 collective-permute-done.received_ref
  79.6 0.1 add.2
  79.7 1.6 %collective-permute-start.1 = (bf16[256,512]{1,0:T(8,128)(2,1)S(1)}, bf16[256,512]{1,0:T(8,128)(2,1)S(1)}, u32[]{:S(2)}, u32[]{:S(2)}) collective-permute-start(bf16[256,512]{1,0:T(8,128)(2,1)S(1)} %add.2), channel_id=1, source_target_pairs={{0,2},{1,3},{2,0},{3,1},{4,6},{5,7},{6,4},{7,5},{8,10},{9,11},{10,... | collective-permute-start | bytes 786440 | tf_op jit(solution)/shard_map/ppermute | solution.py:406
  81.3 6.8 %collective-permute-done.1 = bf16[256,512]{1,0:T(8,128)(2,1)S(1)} collective-permute-done((bf16[256,512]{1,0:T(8,128)(2,1)S(1)}, bf16[256,512]{1,0:T(8,128)(2,1)S(1)}, u32[]{:S(2)}, u32[]{:S(2)}) %collective-permute-start.1) | collective-permute-done | bytes 262176 | tf_op jit(solution)/shard_map/ppermute | solution.py:406
  88.1 0.1 add_mixed.1
  88.2 1.9 %collective-permute-start.5 = (bf16[32,512]{1,0:T(8,128)(2,1)S(1)}, bf16[32,512]{1,0:T(8,128)(2,1)S(1)}, u32[]{:S(2)}, u32[]{:S(2)}) collective-permute-start(bf16[32,512]{1,0:T(8,128)(2,1)S(1)} %get-tuple-element.41), channel_id=1, source_target_pairs={{0,4},{4,0},{8,12},{12,8},{16,20},{20,16},{24,28},{28,24},{1,5},{5... | collective-permute-start | bytes 98312 | tf_op jit(solution)/shard_map/ppermute | solution.py:479
  90.1 1.5 %collective-permute-start.6 = (bf16[32,512]{1,0:T(8,128)(2,1)S(1)}, bf16[32,512]{1,0:T(8,128)(2,1)S(1)}, u32[]{:S(2)}, u32[]{:S(2)}) collective-permute-start(bf16[32,512]{1,0:T(8,128)(2,1)S(1)} %get-tuple-element.42), channel_id=1, source_target_pairs={{0,8},{4,12},{8,0},{12,4},{16,24},{20,28},{24,16},{28,20},{1,9},{5... | collective-permute-start | bytes 98312 | tf_op jit(solution)/shard_map/ppermute | solution.py:479
  91.6 0.2 collective-permute-start.7
  91.7 2.8 %collective-permute-start.8 = (bf16[32,512]{1,0:T(8,128)(2,1)S(1)}, bf16[32,512]{1,0:T(8,128)(2,1)S(1)}, u32[]{:S(2)}, u32[]{:S(2)}) collective-permute-start(bf16[32,512]{1,0:T(8,128)(2,1)S(1)} %get-tuple-element.44), channel_id=1, source_target_pairs={{0,16},{4,20},{8,24},{12,28},{16,0},{20,4},{24,8},{28,12},{1,17},{... | collective-permute-start | bytes 98312 | tf_op jit(solution)/shard_map/ppermute | solution.py:479
  94.5 1.4 %collective-permute-start.9 = (bf16[32,512]{1,0:T(8,128)(2,1)S(1)}, bf16[32,512]{1,0:T(8,128)(2,1)S(1)}, u32[]{:S(2)}, u32[]{:S(2)}) collective-permute-start(bf16[32,512]{1,0:T(8,128)(2,1)S(1)} %get-tuple-element.45), channel_id=1, source_target_pairs={{0,20},{4,16},{8,28},{12,24},{16,4},{20,0},{24,12},{28,8},{1,21},{... | collective-permute-start | bytes 98312 | tf_op jit(solution)/shard_map/ppermute | solution.py:479
  96.0 3.3 %collective-permute-start.10 = (bf16[32,512]{1,0:T(8,128)(2,1)S(1)}, bf16[32,512]{1,0:T(8,128)(2,1)S(1)}, u32[]{:S(2)}, u32[]{:S(2)}) collective-permute-start(bf16[32,512]{1,0:T(8,128)(2,1)S(1)} %get-tuple-element.46), channel_id=1, source_target_pairs={{0,24},{4,28},{8,16},{12,20},{16,8},{20,12},{24,0},{28,4},{1,25},{... | collective-permute-start | bytes 98312 | tf_op jit(solution)/shard_map/ppermute | solution.py:479
  99.3 0.4 collective-permute-start.11
  99.7 0.9 collective-permute-done.9.refs_5_
  100.6 1.4 %collective-permute-done.10.refs_6_ = bf16[32,512]{1,0:T(8,128)(2,1)S(1)} collective-permute-done((bf16[32,512]{1,0:T(8,128)(2,1)S(1)}, bf16[32,512]{1,0:T(8,128)(2,1)S(1)}, u32[]{:S(2)}, u32[]{:S(2)}) %collective-permute-start.10) | collective-permute-done | bytes 32800 | tf_op jit(solution)/shard_map/ppermute | solution.py:479
  102.0 4.0 %collective-permute-done.11.refs_7_ = bf16[32,512]{1,0:T(8,128)(2,1)S(1)} collective-permute-done((bf16[32,512]{1,0:T(8,128)(2,1)S(1)}, bf16[32,512]{1,0:T(8,128)(2,1)S(1)}, u32[]{:S(2)}, u32[]{:S(2)}) %collective-permute-start.11) | collective-permute-done | bytes 32800 | tf_op jit(solution)/shard_map/ppermute | solution.py:479
  106.0 0.1 collective-permute-start.12
  106.1 0.0 all-gather.5.cloned.1.call-done
  106.1 12.1 %all-gather.7.cloned.1.call-done = bf16[64,32,256]{2,1,0:T(8,128)(2,1)} async-done(((bf16[8,32,256]{2,1,0:T(8,128)(2,1)}), bf16[64,32,256]{2,1,0:T(8,128)(2,1)}) %all-gather.7.cloned.1.call-update) | async-done | bytes 1048592 | tf_op jit(solution)/shard_map/all_gather | solution.py:504
  118.2 1.2 copy-done.2
  119.5 1.2 copy-done.3
  120.7 0.7 mix_gradient.1
  121.4 0.1 collective-permute-start.14
  121.5 1.0 make_output.1
  122.6 0.9 make_gradient.1
  123.5 0.8 place.1
  (20 shorter events, 0.1 us)
Async XLA Ops:
  9.2 27.1 %copy-start.5 = (s32[2,16]{1,0:T(2,128)S(1)}, s32[2,16]{1,0:T(2,128)}, u32[]{:S(2)}) copy-start(s32[2,16]{1,0:T(2,128)} %mask_ref.1) | copy-start | bytes 388
  9.2 21.9 %all-to-all-start = ((bf16[8,32,1024]{2,1,0:T(8,128)(2,1)}), bf16[8,32,1024]{2,1,0:T(8,128)(2,1)S(1)}, u32[]{:S(2)}, u32[]{:S(2)}) async-start(bf16[8,32,1024]{2,1,0:T(8,128)(2,1)} %get-tuple-element.28), calls=%async_computation | async-start | bytes 1048576 | tf_op jit(solution)/shard_map/all_to_all | solution.py:402
  16.6 89.5 %all-gather.5.cloned.1.call-start = ((), (), s32[]{:S(2)}) async-start(), calls=%async_computation.4 | async-start | bytes 1179648 | tf_op jit(solution)/shard_map/all_gather | solution.py:504
  16.6 1.6 %collective-permute-start.2 = (bf16[8,32,512]{2,1,0:T(8,128)(2,1)S(1)}, bf16[8,32,512]{2,1,0:T(8,128)(2,1)S(1)}, u32[]{:S(2)}, u32[]{:S(2)}) collective-permute-start(bf16[8,32,512]{2,1,0:T(8,128)(2,1)S(1)} %get-tuple-element.32), channel_id=1, source_target_pairs={{0,1},{1,0},{2,3},{3,2},{4,5},{5,4},{6,7},{7,6},{8,9},{9,8},{10,11... | collective-permute-start | bytes 786440 | tf_op jit(solution)/shard_map/ppermute | solution.py:406
  18.3 8.4 %collective-permute-start.3 = (bf16[8,32,512]{2,1,0:T(8,128)(2,1)S(1)}, bf16[8,32,512]{2,1,0:T(8,128)(2,1)S(1)}, u32[]{:S(2)}, u32[]{:S(2)}) collective-permute-start(bf16[8,32,512]{2,1,0:T(8,128)(2,1)S(1)} %add.3.own_ref), channel_id=1, source_target_pairs={{0,2},{1,3},{2,0},{3,1},{4,6},{5,7},{6,4},{7,5},{8,10},{9,11},{10,... | collective-permute-start | bytes 786440 | tf_op jit(solution)/shard_map/ppermute | solution.py:406
  31.9 14.1 %all-to-all-start.1 = ((bf16[8,32,512]{2,1,0:T(8,128)(2,1)}), bf16[8,32,512]{2,1,0:T(8,128)(2,1)S(1)}, u32[]{:S(2)}, u32[]{:S(2)}) async-start(bf16[8,32,512]{2,1,0:T(8,128)(2,1)} %get-tuple-element.33), calls=%async_computation.1 | async-start | bytes 524288 | tf_op jit(solution)/shard_map/all_to_all | solution.py:402
  35.6 82.6 %all-gather.7.cloned.1.call-start = ((), (), s32[]{:S(2)}) async-start(), calls=%async_computation.5 | async-start | bytes 1179648 | tf_op jit(solution)/shard_map/all_gather | solution.py:504
  46.1 28.4 %all-to-all-start.3 = ((bf16[8,256,128]{2,1,0:T(8,128)(2,1)}), bf16[8,256,128]{2,1,0:T(8,128)(2,1)S(1)}, u32[]{:S(2)}, u32[]{:S(2)}) async-start(bf16[8,256,128]{2,1,0:T(8,128)(2,1)} %get-tuple-element.48), calls=%async_computation.3 | async-start | bytes 1048576 | tf_op jit(solution)/shard_map/all_to_all | solution.py:402
  52.0 1.5 %collective-permute-start.4 = (bf16[256,512]{1,0:T(8,128)(2,1)S(1)}, bf16[256,512]{1,0:T(8,128)(2,1)S(1)}, u32[]{:S(2)}, u32[]{:S(2)}) collective-permute-start(bf16[256,512]{1,0:T(8,128)(2,1)S(1)} %bitcast.27), channel_id=1, source_target_pairs={{0,1},{1,0},{2,3},{3,2},{4,5},{5,4},{6,7},{7,6},{8,9},{9,8},{10,11... | collective-permute-start | bytes 786440 | tf_op jit(solution)/shard_map/ppermute | solution.py:406
  74.5 48.0 %all-to-all-start.2 = ((bf16[8,32,1024]{2,1,0:T(8,128)(2,1)}), bf16[8,32,1024]{2,1,0:T(8,128)(2,1)S(1)}, u32[]{:S(2)}, u32[]{:S(2)}) async-start(bf16[8,32,1024]{2,1,0:T(8,128)(2,1)} %bitcast.9), calls=%async_computation.2 | async-start | bytes 1048576 | tf_op jit(solution)/shard_map/all_to_all | solution.py:402
  78.0 1.6 %collective-permute-start = (bf16[256,512]{1,0:T(8,128)(2,1)S(1)}, bf16[256,512]{1,0:T(8,128)(2,1)S(1)}, u32[]{:S(2)}, u32[]{:S(2)}) collective-permute-start(bf16[256,512]{1,0:T(8,128)(2,1)S(1)} %get-tuple-element.30), channel_id=1, source_target_pairs={{0,1},{1,0},{2,3},{3,2},{4,5},{5,4},{6,7},{7,6},{8,9},{9,8},{10,11... | collective-permute-start | bytes 786440 | tf_op jit(solution)/shard_map/ppermute | solution.py:406
  78.1 28.0 %collective-permute-start.13 = (bf16[8,256,128]{2,1,0:T(8,128)(2,1)S(1)}, bf16[8,256,128]{2,1,0:T(8,128)(2,1)S(1)}, u32[]{:S(2)}, u32[]{:S(2)}) collective-permute-start(bf16[8,256,128]{2,1,0:T(8,128)(2,1)S(1)} %all-to-all-done.3.own_ref), channel_id=1, source_target_pairs={{0,1},{1,0},{2,3},{3,2},{4,5},{5,4},{6,7},{7,6},{8,9},{9,8},{10,11... | collective-permute-start | bytes 1572872 | tf_op jit(solution)/shard_map/ppermute | solution.py:406
  79.7 8.4 %collective-permute-start.1 = (bf16[256,512]{1,0:T(8,128)(2,1)S(1)}, bf16[256,512]{1,0:T(8,128)(2,1)S(1)}, u32[]{:S(2)}, u32[]{:S(2)}) collective-permute-start(bf16[256,512]{1,0:T(8,128)(2,1)S(1)} %add.2), channel_id=1, source_target_pairs={{0,2},{1,3},{2,0},{3,1},{4,6},{5,7},{6,4},{7,5},{8,10},{9,11},{10,... | collective-permute-start | bytes 786440 | tf_op jit(solution)/shard_map/ppermute | solution.py:406
  88.2 33.4 %copy-start = (bf16[2,1,2,64,1024]{4,3,2,1,0:T(8,128)(2,1)S(1)}, bf16[2,1,2,64,1024]{4,3,2,1,0:T(8,128)(2,1)}, u32[]{:S(2)}) copy-start(bf16[2,1,2,64,1024]{4,3,2,1,0:T(8,128)(2,1)} %param.6) | copy-start | bytes 1572868
  88.2 33.4 %copy-start.4 = (f32[1,1024]{1,0:T(1,128)S(1)}, f32[1,1024]{1,0:T(1,128)}, u32[]{:S(2)}) copy-start(f32[1,1024]{1,0:T(1,128)} %gain_ref.3) | copy-start | bytes 12292
  88.2 6.3 %collective-permute-start.5 = (bf16[32,512]{1,0:T(8,128)(2,1)S(1)}, bf16[32,512]{1,0:T(8,128)(2,1)S(1)}, u32[]{:S(2)}, u32[]{:S(2)}) collective-permute-start(bf16[32,512]{1,0:T(8,128)(2,1)S(1)} %get-tuple-element.41), channel_id=1, source_target_pairs={{0,4},{4,0},{8,12},{12,8},{16,20},{20,16},{24,28},{28,24},{1,5},{5... | collective-permute-start | bytes 98312 | tf_op jit(solution)/shard_map/ppermute | solution.py:479
  90.1 5.9 %collective-permute-start.6 = (bf16[32,512]{1,0:T(8,128)(2,1)S(1)}, bf16[32,512]{1,0:T(8,128)(2,1)S(1)}, u32[]{:S(2)}, u32[]{:S(2)}) collective-permute-start(bf16[32,512]{1,0:T(8,128)(2,1)S(1)} %get-tuple-element.42), channel_id=1, source_target_pairs={{0,8},{4,12},{8,0},{12,4},{16,24},{20,28},{24,16},{28,20},{1,9},{5... | collective-permute-start | bytes 98312 | tf_op jit(solution)/shard_map/ppermute | solution.py:479
  91.6 7.7 %collective-permute-start.7 = (bf16[32,512]{1,0:T(8,128)(2,1)S(1)}, bf16[32,512]{1,0:T(8,128)(2,1)S(1)}, u32[]{:S(2)}, u32[]{:S(2)}) collective-permute-start(bf16[32,512]{1,0:T(8,128)(2,1)S(1)} %get-tuple-element.43), channel_id=1, source_target_pairs={{0,12},{4,8},{8,4},{12,0},{16,28},{20,24},{24,20},{28,16},{1,13},{... | collective-permute-start | bytes 98312 | tf_op jit(solution)/shard_map/ppermute | solution.py:479
  91.7 7.9 %collective-permute-start.8 = (bf16[32,512]{1,0:T(8,128)(2,1)S(1)}, bf16[32,512]{1,0:T(8,128)(2,1)S(1)}, u32[]{:S(2)}, u32[]{:S(2)}) collective-permute-start(bf16[32,512]{1,0:T(8,128)(2,1)S(1)} %get-tuple-element.44), channel_id=1, source_target_pairs={{0,16},{4,20},{8,24},{12,28},{16,0},{20,4},{24,8},{28,12},{1,17},{... | collective-permute-start | bytes 98312 | tf_op jit(solution)/shard_map/ppermute | solution.py:479
  94.5 6.1 %collective-permute-start.9 = (bf16[32,512]{1,0:T(8,128)(2,1)S(1)}, bf16[32,512]{1,0:T(8,128)(2,1)S(1)}, u32[]{:S(2)}, u32[]{:S(2)}) collective-permute-start(bf16[32,512]{1,0:T(8,128)(2,1)S(1)} %get-tuple-element.45), channel_id=1, source_target_pairs={{0,20},{4,16},{8,28},{12,24},{16,4},{20,0},{24,12},{28,8},{1,21},{... | collective-permute-start | bytes 98312 | tf_op jit(solution)/shard_map/ppermute | solution.py:479
  96.0 6.1 %collective-permute-start.10 = (bf16[32,512]{1,0:T(8,128)(2,1)S(1)}, bf16[32,512]{1,0:T(8,128)(2,1)S(1)}, u32[]{:S(2)}, u32[]{:S(2)}) collective-permute-start(bf16[32,512]{1,0:T(8,128)(2,1)S(1)} %get-tuple-element.46), channel_id=1, source_target_pairs={{0,24},{4,28},{8,16},{12,20},{16,8},{20,12},{24,0},{28,4},{1,25},{... | collective-permute-start | bytes 98312 | tf_op jit(solution)/shard_map/ppermute | solution.py:479
  99.3 6.7 %collective-permute-start.11 = (bf16[32,512]{1,0:T(8,128)(2,1)S(1)}, bf16[32,512]{1,0:T(8,128)(2,1)S(1)}, u32[]{:S(2)}, u32[]{:S(2)}) collective-permute-start(bf16[32,512]{1,0:T(8,128)(2,1)S(1)} %get-tuple-element.47), channel_id=1, source_target_pairs={{0,28},{4,24},{8,20},{12,16},{16,12},{20,8},{24,4},{28,0},{1,29},{... | collective-permute-start | bytes 98312 | tf_op jit(solution)/shard_map/ppermute | solution.py:479
  106.0 15.5 %collective-permute-start.12 = (bf16[8,32,512]{2,1,0:T(8,128)(2,1)S(1)}, bf16[8,32,512]{2,1,0:T(8,128)(2,1)S(1)}, u32[]{:S(2)}, u32[]{:S(2)}) collective-permute-start(bf16[8,32,512]{2,1,0:T(8,128)(2,1)S(1)} %join.1.own_ref), channel_id=1, source_target_pairs={{0,1},{1,0},{2,3},{3,2},{4,5},{5,4},{6,7},{7,6},{8,9},{9,8},{10,11... | collective-permute-start | bytes 786440 | tf_op jit(solution)/shard_map/ppermute | solution.py:406
  118.2 1.2 copy-start.2
  119.5 1.2 copy-start.3
  120.7 1.9 %copy-start.1 = (bf16[2,1,2,64,1024]{4,3,2,1,0:T(8,128)(2,1)S(1)}, bf16[2,1,2,64,1024]{4,3,2,1,0:T(8,128)(2,1)}, u32[]{:S(2)}) copy-start(bf16[2,1,2,64,1024]{4,3,2,1,0:T(8,128)(2,1)} %param.11) | copy-start | bytes 1572868
  121.4 2.0 %collective-permute-start.14 = (bf16[128,512]{1,0:T(8,128)(2,1)S(1)}, bf16[128,512]{1,0:T(8,128)(2,1)S(1)}, u32[]{:S(2)}, u32[]{:S(2)}) collective-permute-start(bf16[128,512]{1,0:T(8,128)(2,1)S(1)} %get-tuple-element.52), channel_id=1, source_target_pairs={{0,1},{1,0},{2,3},{3,2},{4,5},{5,4},{6,7},{7,6},{8,9},{9,8},{10,11... | collective-permute-start | bytes 393224 | tf_op jit(solution)/shard_map/ppermute | solution.py:406
Sparse Core Ops, SparseCore 0:
  32.1 42.9 all-gather.4
  77.2 41.0 all-gather.6

commit v3 on v0

--- a/solution.py
+++ b/solution.py
@@ -44,6 +44,10 @@
     half = width // 2
     core = lax.axis_index("lev") % 2
     return pl.ds(pl.multiple_of((core ^ which) * half, half), half)
+
+
+def in_hbm(array):
+    return pltpu.with_memory_space_constraint(array, pltpu.HBM)
 
 
 def call(kernel, name, out_shape, *operands):
@@ -78,9 +82,9 @@
         "pack",
         [jax.ShapeDtypeStruct(shape + (width,), BF16)]
         + [jax.ShapeDtypeStruct(shape + (width // 2,), BF16)] * 2,
-        tokens,
-        cot,
-        gain,
+        in_hbm(tokens),
+        in_hbm(cot),
+        in_hbm(gain),
     )
 
 
@@ -89,13 +93,13 @@
     for s, ref in enumerate((own_ref, other_ref)):
         cols = half_cols(s, width)
         gain = gain_ref[:, cols]
-        for b in range(batch):
-            for q in range(parts):
-                for r in range(rows):
-                    mixed = ref[b * parts + q, r * chunk : (r + 1) * chunk, :].astype(F32)
-                    out_ref[b, r, q, :, cols] = (
-                        tok_ref[b, r, q, :, cols].astype(F32) + gain * mixed
-                    ).astype(BF16)
+        for t in range(batch * parts):
+            b, q = t // parts, t % parts
+            for r in range(rows):
+                mixed = ref[t, r * chunk : (r + 1) * chunk, :].astype(F32)
+                out_ref[b, r, q, :, cols] = (
+                    tok_ref[b, r, q, :, cols].astype(F32) + gain * mixed
+                ).astype(BF16)
 
 
 def make_output(tokens, gain, mixed):
@@ -114,7 +118,7 @@
     for b in range(batch):
         for q in range(parts):
             for r in range(rows):
-                back = back_ref[b * parts + q, r * chunk : (r + 1) * chunk, :].astype(F32)
+                back = back_ref[b * parts + q, r * chunk : (r + 1) * chunk, :width].astype(F32)
                 out_ref[b, r, q] = (cot_ref[b, r, q].astype(F32) + back).astype(BF16)
 
 
@@ -124,10 +128,25 @@
     )
 
 
+def by_head(tile, lane):
+    zero = jnp.zeros_like(tile)
+    return jnp.concatenate([jnp.where(lane == 0, tile, zero), jnp.where(lane == 1, tile, zero)], axis=0)
+
+
+def one_head(stacked, lane):
+    count = lane.shape[0]
+    return jnp.where(lane == 0, stacked[:count], stacked[count:])
+
+
+def side_by_side(stacked):
+    count = stacked.shape[0] // 2
+    return jnp.concatenate([stacked[:count], stacked[count:]], axis=1)
+
+
 def forward_kernel(
     samples, lat_count, chunk, owners,
     tok_ref, mask_ref, wq_ref, wk_ref, wv_ref, wm_ref,
-    qn_ref, kn_ref, v_ref, rq_ref, rk_ref, p_ref, att_ref, own_ref, other_ref,
+    qn_ref, kn_ref, v_ref, rq_ref, rk_ref, ri_ref, p_ref, att_ref, own_ref, other_ref,
     normed_ref, acc_ref, keep_ref,
 ):
     step = pl.program_id(0)
@@ -166,24 +185,23 @@
     qn_ref[...] = qn
     kn_ref[...] = kn
     v_ref[...] = v
-    rq_ref[...] = rq
-    rk_ref[...] = rk
+    rq_ref[...] = rq.astype(BF16)
+    rk_ref[...] = rk.astype(BF16)
     keep = keep_ref[...]
+    keep = jnp.concatenate([keep, keep], axis=0)
     lane = lax.broadcasted_iota(jnp.int32, (count, 128), 1) // head_width
-    per_tile = 128 // head_width
+    ones = jnp.ones((count, 128), BF16)
     tiles = []
     for t in range(GROUP // 128):
         cols = slice(t * 128, (t + 1) * 128)
-        q_t, k_t, v_t = qn[:, cols], kn[:, cols], v[:, cols]
-        total = None
-        for h in range(per_tile):
-            q_h = jnp.where(lane == h, q_t * score_scale, jnp.zeros_like(q_t))
-            e = jnp.exp(nt(q_h, k_t)) * keep
-            p = (e * (1.0 / jnp.sum(e, axis=-1, keepdims=True))).astype(BF16)
-            p_ref[t * per_tile + h] = p
-            o = nn(p, v_t)
-            total = o if total is None else jnp.where(lane == h, o, total)
-        tiles.append(total)
+        v_ones = jnp.concatenate([v[:, cols], ones], axis=1)
+        e = jnp.exp(nt(by_head(qn[:, cols] * score_scale, lane), kn[:, cols])) * keep
+        e = e.astype(BF16)
+        p_ref[t] = e
+        o = nn(e, v_ones)
+        inverse = 1.0 / o[:, 128:]
+        tiles.append(one_head(o[:, :128] * inverse, lane))
+        ri_ref[:, cols] = one_head(inverse, lane)
     att = jnp.concatenate(tiles, axis=1).astype(BF16)
     features = att_ref.shape[-1]
     for f in range(GROUP // features):
@@ -200,7 +218,6 @@
     count, width = tok_col.shape
     samples, lat_count = key_mask.shape
     steps = width // GROUP
-    per_step = GROUP // (width // HEADS)
     features = width // owners
     same = lambda shape: pl.BlockSpec(shape, lambda i: (0, 0))
     cols = pl.BlockSpec((count, GROUP), lambda i: (0, i))
@@ -208,9 +225,9 @@
     return pl.pallas_call(
         functools.partial(forward_kernel, samples, lat_count, chunk, owners),
         out_shape=(
-            [jax.ShapeDtypeStruct((count, width), BF16)] * 3
-            + [jax.ShapeDtypeStruct((count, width), F32)] * 2
-            + [jax.ShapeDtypeStruct((HEADS, count, count), BF16)]
+            [pltpu.HBM((count, width), BF16)] * 5
+            + [pltpu.HBM((count, width), F32)]
+            + [pltpu.HBM((width // 128, 2 * count, count), BF16)]
             + [jax.ShapeDtypeStruct((owners, count, features), BF16)]
             + [jax.ShapeDtypeStruct((count, width // 2), BF16)] * 2
         ),
@@ -224,8 +241,8 @@
             pl.BlockSpec((GROUP, width), lambda i: (i, 0)),
         ],
         out_specs=(
-            [cols] * 5
-            + [pl.BlockSpec((per_step, count, count), lambda i: (i, 0, 0))]
+            [cols] * 6
+            + [pl.BlockSpec((GROUP // 128, 2 * count, count), lambda i: (i, 0, 0))]
             + [pl.BlockSpec((GROUP // features, count, features), lambda i: (i, 0, 0))]
             + [same((count, width // 2))] * 2
         ),
@@ -241,12 +258,12 @@
             transcendentals=HEADS * count * count,
         ),
         name="forward",
-    )(tok_col, key_mask, w_qkv, w_qkv, w_qkv, w_mix)
+    )(tok_col, key_mask, *[in_hbm(w_qkv)] * 3, in_hbm(w_mix))
 
 
 def backward_kernel(
     tok_ref, own_ref, other_ref, wm_ref, wq_ref, wk_ref, wv_ref,
-    qn_ref, kn_ref, v_ref, rq_ref, rk_ref, p_ref,
+    qn_ref, kn_ref, v_ref, rq_ref, rk_ref, ri_ref, p_ref, _,
     out_ref, acc_ref,
 ):
     step = pl.program_id(0)
@@ -254,32 +271,28 @@
     head_width = width // HEADS
     d_att = nt(own_ref[...], wm_ref[:, half_cols(0, width)])
     d_att += nt(other_ref[...], wm_ref[:, half_cols(1, width)])
-    d_att = d_att.astype(BF16)
+    inverse = ri_ref[...]
+    d_att = (d_att * inverse).astype(BF16)
     qn, kn, v = qn_ref[...], kn_ref[...], v_ref[...]
     lane = lax.broadcasted_iota(jnp.int32, (count, 128), 1) // head_width
-    per_tile = 128 // head_width
     dq_tiles, dk_tiles, dv_tiles = [], [], []
     for t in range(GROUP // 128):
         cols = slice(t * 128, (t + 1) * 128)
-        q_t, k_t, v_t, d_t = qn[:, cols], kn[:, cols], v[:, cols], d_att[:, cols]
-        dq = dk = dv = None
-        for h in range(per_tile):
-            d_h = jnp.where(lane == h, d_t, jnp.zeros_like(d_t))
-            d_p = nt(d_h, v_t)
-            p_b = p_ref[t * per_tile + h]
-            p = p_b.astype(F32)
-            pd = p * d_p
-            d_s = ((pd - p * jnp.sum(pd, axis=-1, keepdims=True)) * score_scale).astype(BF16)
-            dq_h, dk_h, dv_h = nn(d_s, k_t), tn(d_s, q_t), tn(p_b, d_t)
-            if dq is None:
-                dq, dk, dv = dq_h, dk_h, dv_h
-            else:
-                dq = jnp.where(lane == h, dq_h, dq)
-                dk = jnp.where(lane == h, dk_h, dk)
-                dv = jnp.where(lane == h, dv_h, dv)
-        dq_tiles.append(dq)
-        dk_tiles.append(dk)
-        dv_tiles.append(dv)
+        d_t = d_att[:, cols]
+        d_p = nt(by_head(d_t, lane), v[:, cols])
+        e = p_ref[t]
+        e_wide = e.astype(F32)
+        first = t * 128
+        second = first + head_width
+        row_inverse = jnp.concatenate(
+            [inverse[:, first : first + 1], inverse[:, second : second + 1]], axis=0
+        )
+        weighted = e_wide * d_p
+        inner = jnp.sum(weighted, axis=-1, keepdims=True) * row_inverse
+        d_s = (weighted - e_wide * inner).astype(BF16)
+        dq_tiles.append(one_head(nn(d_s, kn[:, cols]), lane) * score_scale)
+        dk_tiles.append(one_head(tn(side_by_side(d_s), qn[:, cols]), lane) * score_scale)
+        dv_tiles.append(one_head(tn(side_by_side(e), d_t), lane))
     mean_mat = block_mean(head_width)
     dq = jnp.concatenate(dq_tiles, axis=1)
     dk = jnp.concatenate(dk_tiles, axis=1)
@@ -288,7 +301,7 @@
     def through_norm(upstream, unit, factor):
         unit = unit.astype(F32)
         inner = nn((upstream * unit).astype(BF16), mean_mat)
-        return (factor * (upstream - unit * inner)).astype(BF16)
+        return (factor.astype(F32) * (upstream - unit * inner)).astype(BF16)
 
     gq = through_norm(dq, qn, rq_ref[...])
     gk = through_norm(dk, kn, rk_ref[...])
@@ -311,10 +324,9 @@
         out_ref[...] = (rx * d - x * (rx * rx * rx * inner)).astype(BF16)
 
 
-def backward(tok_col, flow, w_mix, w_qkv, saved):
+def backward(tok_col, flow, w_mix, w_qkv, saved, after):
     count, width = tok_col.shape
     steps = width // GROUP
-    per_step = GROUP // (width // HEADS)
     same = lambda shape: pl.BlockSpec(shape, lambda i: (0, 0))
     cols = pl.BlockSpec((count, GROUP), lambda i: (0, i))
     weight = lambda which: pl.BlockSpec((width, GROUP), lambda i: (0, i + which * steps))
@@ -330,8 +342,9 @@
             weight(0),
             weight(1),
             weight(2),
-            *([cols] * 5),
-            pl.BlockSpec((per_step, count, count), lambda i: (i, 0, 0)),
+            *([cols] * 6),
+            pl.BlockSpec((GROUP // 128, 2 * count, count), lambda i: (i, 0, 0)),
+            pl.BlockSpec(memory_space=pl.ANY),
         ],
         out_specs=same((count, width)),
         scratch_shapes=[pltpu.VMEM((count, width), F32)],
@@ -342,7 +355,7 @@
             transcendentals=0,
         ),
         name="backward",
-    )(tok_col, *flow, w_mix, w_qkv, w_qkv, w_qkv, *saved)
+    )(tok_col, *flow, in_hbm(w_mix), *[in_hbm(w_qkv)] * 3, *map(in_hbm, saved), after)
 
 
 def mix_gradient_kernel(factor, own_ref, other_ref, flow_ref, own_out, other_out, flow_scr):
@@ -399,16 +412,62 @@
     return lax.ppermute(block, "lev", [(i, i ^ offset) for i in range(lax.axis_size("lev"))])
 
 
-def level_total(own, other):
-    total = own
-    received = from_level(other, 1)
-    offset = 1
-    while True:
-        total = (total.astype(F32) + received.astype(F32)).astype(BF16)
+def add_kernel(own_ref, received_ref, out_ref):
+    out_ref[...] = (own_ref[...].astype(F32) + received_ref[...].astype(F32)).astype(BF16)
+
+
+def add(own, received):
+    return call(add_kernel, "add", jax.ShapeDtypeStruct(own.shape, BF16), own, received)
+
+
+def pair_total(own, other):
+    return add(own, from_level(other, 1))
+
+
+def before_last(total):
+    offset = 2
+    while 2 * offset < lax.axis_size("lev"):
+        total = add(total, from_level(total, offset))
         offset *= 2
-        if offset == lax.axis_size("lev"):
-            return total
-        received = from_level(total, offset)
+    return total, from_level(total, offset)
+
+
+def add_flow_kernel(own_ref, received_ref, _, out_ref):
+    add_kernel(own_ref, received_ref, out_ref)
+
+
+def add_flow(own, received, after):
+    whole = pl.BlockSpec(memory_space=pltpu.VMEM)
+    return pl.pallas_call(
+        add_flow_kernel,
+        out_shape=jax.ShapeDtypeStruct(own.shape, BF16),
+        in_specs=[whole, whole, pl.BlockSpec(memory_space=pl.ANY)],
+        out_specs=whole,
+        compiler_params=params(),
+        name="add_flow",
+    )(own, received, after)
+
+
+def add_mixed_kernel(own_ref, received_ref, back_ref, out_ref):
+    width = back_ref.shape[-1]
+    out_ref[:, :width] = back_ref[...]
+    out_ref[:, width:] = (own_ref[...].astype(F32) + received_ref[...].astype(F32)).astype(BF16)
+
+
+def add_mixed(own, received, back):
+    count, width = back.shape
+    shape = jax.ShapeDtypeStruct((count, width + own.shape[-1]), BF16)
+    return call(add_mixed_kernel, "add_mixed", shape, own, received, back)
+
+
+def cut_kernel(in_ref, out_ref):
+    out_ref[...] = in_ref[:, :, in_ref.shape[-1] - out_ref.shape[-1] :]
+
+
+def cut_mixed(received):
+    owners, cells, wide = received.shape
+    shape = jax.ShapeDtypeStruct((owners, cells, wide // 3), BF16)
+    return call(cut_kernel, "cut_mixed", shape, received)
 
 
 def on_device(tokens, key_mask, w_qkv, w_mix, level_scale, cotangent):
@@ -425,7 +484,7 @@
 
     tok_send, cot_own, cot_other = pack(tok_band, cot_band, level_scale)
     tok_col = swap(tok_send).reshape(count, width)
-    flow_band = level_total(cot_own, cot_other)
+    flow_band = add_flow(*before_last(pair_total(cot_own, cot_other)), tok_col)
     flow_own = swap(flow_band).reshape(count, half)
     flow = (flow_own, from_level(flow_own, 1))
     flow_all = lax.all_gather(flow_band, "lat", axis=0)
@@ -434,12 +493,12 @@
         tok_col, key_mask, w_qkv, w_mix, chunk, owners
     )
     attended = swap(attended)
-    mix_half = level_total(mix_own, mix_other)
-    back_col = backward(tok_col, flow, w_mix, w_qkv, saved)
-    back = swap(back_col.reshape(owners, cells, width))
-    mix_band = swap(mix_half.reshape(owners, cells, half))
+    mix_terms = before_last(pair_total(mix_own, mix_other))
+    back_col = backward(tok_col, flow, w_mix, w_qkv, saved, mix_terms[0])
+    back = swap(add_mixed(*mix_terms, back_col).reshape(owners, cells, width + half))
+    d_tokens = make_gradient(cot_band, back)
+    mix_band = cut_mixed(back)
     output = make_output(tok_band, level_scale, (mix_band, from_level(mix_band, 1)))
-    d_tokens = make_gradient(cot_band, back)
 
     factor = 1.0 / math.sqrt(count * owners)
     grad_own, grad_other = mix_gradient(attended, from_level(attended, 1), flow_all, factor)

time: 151 us -> 114 us (0.75)
  blocking collectives: 28.2 us -> 0 us
  local copies, waits for them, and re-layouts: 26.4 us -> 1.6 us
  waiting for transfers between devices: 26.5 us -> 41 us
  Pallas kernels: 27.1 us -> 32.1 us
  other arithmetic: 2.69 us -> 0 us
    all_to_all x1 -> x0, blocking collectives: 28.2 us -> none  [swap(): return lax.all_to_all(block, 'lat', split_axis=0, concat_axis=0, tiled=True)]
    unnamed x54 -> x10, local copies, waits for them, and re-layouts: 26.4 us -> 1.6 us
    all_to_all x4, waiting for transfers between devices: 10.4 us -> 31.5 us  [swap(): return lax.all_to_all(block, 'lat', split_axis=0, concat_axis=0, tiled=True)]
    ppermute x8, waiting for transfers between devices: 16.1 us -> 9.39 us  [from_level(): lax.ppermute(block, 'lev', [(i, i ^ offset) for i in range(lax.axis_size(...]
    convert_element_type x4 -> x0, other arithmetic: 2.69 us -> none  [level_total(): total = (total.astype(F32) + received.astype(F32)).astype(BF16)]
    pallas_call x4 -> x8, Pallas kernels: 3.81 us -> 5.9 us  [call(): pl.pallas_call(kernel, out_shape=out_shape, compiler_params=params(), nam...]
  transfers between devices with their start and end apart: 13 -> 13, of which waited for: 6 -> 7; matrix products, arithmetic and copies ran while one was open for 1% -> 0% of each run, Pallas kernels for 17% -> 25%
where the time goes in v3:
time: 114 us; the launch traced here: 113 us
  waiting for transfers between devices  41 us (36%)
  Pallas kernels  32.1 us (28%)
  starting transfers between devices  24.7 us (22%)
  between operations  14.1 us (12%)
  local copies, waits for them, and re-layouts  1.6 us (1%)
    all_to_all x4, waiting for transfers between devices, swap(): return lax.all_to_all(block, 'lat', split_axis=0, concat_axis=0, tiled=True)  31.5 us
    all_to_all x4, starting transfers between devices, swap(): return lax.all_to_all(block, 'lat', split_axis=0, concat_axis=0, tiled=True)  20.3 us
    pallas_call x1, Pallas kernels, backward(): pl.pallas_call(backward_kernel, out_shape=jax.ShapeDtypeStruct((count, wi...  15 us
    pallas_call x1, Pallas kernels, forward(): pl.pallas_call(functools.partial(forward_kernel, samples, lat_count, chun...  9.7 us
    ppermute x8, waiting for transfers between devices, from_level(): lax.ppermute(block, 'lev', [(i, i ^ offset) for i in range(lax.axis_size(...  9.39 us
    pallas_call x8, Pallas kernels, call(): pl.pallas_call(kernel, out_shape=out_shape, compiler_params=params(), nam...  5.9 us
    ppermute x8, starting transfers between devices, from_level(): lax.ppermute(block, 'lev', [(i, i ^ offset) for i in range(lax.axis_size(...  4.44 us
  transfers between devices with their start and end apart: 13, of which 7 were waited for; matrix products, arithmetic and copies ran while one was open for 0% of the time, Pallas kernels for 25%

profile of v3, /device:TPU:0, one launch (start us, length us, event | category | flops | bytes accessed | tf_op | source)
XLA Modules:
  0.0 113.5 jit_solution(13160925225623729697)
XLA Ops:
  7.2 2.1 %pack.1 = (bf16[8,32,1024]{2,1,0:T(8,128)(2,1)}, bf16[8,32,512]{2,1,0:T(8,128)(2,1)S(1)}, bf16[8,32,512]{2,1,0:T(8,128)(2,1)S(1)}) custom-call(bf16[2,2,4,16,1024]{4,3,2,1,0:T(8,128)(2,1)} %bitcast.19, bf16[2,2,4,16,1024]{4,3,2,1,0:T(8,128)(2,1)} %bitcast.17, f32[1,1024]{1,0:T(1,128)} %gain_ref.3), custom_call_target="tpu_custom_call" | custom-call | tf_op jit(solution)/shard_map/pack/pallas_call | solution.py:54
  9.2 0.0 copy-start.4
  9.2 7.4 %all-to-all-start = ((bf16[8,32,1024]{2,1,0:T(8,128)(2,1)}), bf16[8,32,1024]{2,1,0:T(8,128)(2,1)S(1)}, u32[]{:S(2)}, u32[]{:S(2)}) async-start(bf16[8,32,1024]{2,1,0:T(8,128)(2,1)} %get-tuple-element.18), calls=%async_computation | async-start | bytes 1048576 | tf_op jit(solution)/shard_map/all_to_all | solution.py:408
  16.6 0.0 all-gather.3.cloned.1.call-start
  16.6 0.1 collective-permute-start.2
  16.7 1.5 %collective-permute-done.2.received_ref = bf16[8,32,512]{2,1,0:T(8,128)(2,1)S(1)} collective-permute-done((bf16[8,32,512]{2,1,0:T(8,128)(2,1)S(1)}, bf16[8,32,512]{2,1,0:T(8,128)(2,1)S(1)}, u32[]{:S(2)}, u32[]{:S(2)}) %collective-permute-start.2) | collective-permute-done | bytes 262176 | tf_op jit(solution)/shard_map/ppermute | solution.py:412
  18.2 0.1 add.3.own_ref
  18.3 1.6 %collective-permute-start.3 = (bf16[8,32,512]{2,1,0:T(8,128)(2,1)S(1)}, bf16[8,32,512]{2,1,0:T(8,128)(2,1)S(1)}, u32[]{:S(2)}, u32[]{:S(2)}) collective-permute-start(bf16[8,32,512]{2,1,0:T(8,128)(2,1)S(1)} %add.3.own_ref), channel_id=1, source_target_pairs={{0,2},{1,3},{2,0},{3,1},{4,6},{5,7},{6,4},{7,5},{8,10},{9,11},{10,... | collective-permute-start | bytes 786440 | tf_op jit(solution)/shard_map/ppermute | solution.py:412
  19.9 6.8 %collective-permute-done.3.received_ref = bf16[8,32,512]{2,1,0:T(8,128)(2,1)S(1)} collective-permute-done((bf16[8,32,512]{2,1,0:T(8,128)(2,1)S(1)}, bf16[8,32,512]{2,1,0:T(8,128)(2,1)S(1)}, u32[]{:S(2)}, u32[]{:S(2)}) %collective-permute-start.3) | collective-permute-done | bytes 262176 | tf_op jit(solution)/shard_map/ppermute | solution.py:412
  26.7 4.4 %all-to-all-done = bf16[8,32,1024]{2,1,0:T(8,128)(2,1)S(1)} async-done(((bf16[8,32,1024]{2,1,0:T(8,128)(2,1)}), bf16[8,32,1024]{2,1,0:T(8,128)(2,1)S(1)}, u32[]{:S(2)}, u32[]{:S(2)}) %all-to-all-start) | async-done | bytes 524320 | tf_op jit(solution)/shard_map/all_to_all | solution.py:408
  31.1 0.8 add_flow.1
  31.9 0.0 all-gather.3.cloned.1.call-update
  31.9 3.6 %all-to-all-start.1 = ((bf16[8,32,512]{2,1,0:T(8,128)(2,1)}), bf16[8,32,512]{2,1,0:T(8,128)(2,1)S(1)}, u32[]{:S(2)}, u32[]{:S(2)}) async-start(bf16[8,32,512]{2,1,0:T(8,128)(2,1)} %add_flow.1), calls=%async_computation.1 | async-start | bytes 524288 | tf_op jit(solution)/shard_map/all_to_all | solution.py:408
  35.5 0.0 copy-done.4
  35.5 9.7 %forward.1 = (bf16[256,1024]{1,0:T(8,128)(2,1)}, bf16[256,1024]{1,0:T(8,128)(2,1)}, bf16[256,1024]{1,0:T(8,128)(2,1)}, bf16[256,1024]{1,0:T(8,128)(2,1)}, bf16[2...) custom-call(bf16[256,1024]{1,0:T(8,128)(2,1)S(1)} %bitcast.15, ...), custom_call_target="tpu_custom_call" | custom-call | flops 3221225472 | bytes 13631488 | tf_op jit(solution)/shard_map/forward/pallas_call | solution.py:225
  45.2 2.0 %all-to-all-done.1 = bf16[8,32,512]{2,1,0:T(8,128)(2,1)S(1)} async-done(((bf16[8,32,512]{2,1,0:T(8,128)(2,1)}), bf16[8,32,512]{2,1,0:T(8,128)(2,1)S(1)}, u32[]{:S(2)}, u32[]{:S(2)}) %all-to-all-start.1) | async-done | bytes 262176 | tf_op jit(solution)/shard_map/all_to_all | solution.py:408
  47.3 4.4 %all-to-all-start.3 = ((bf16[8,256,128]{2,1,0:T(8,128)(2,1)}), bf16[8,256,128]{2,1,0:T(8,128)(2,1)S(1)}, u32[]{:S(2)}, u32[]{:S(2)}) async-start(bf16[8,256,128]{2,1,0:T(8,128)(2,1)} %get-tuple-element.30), calls=%async_computation.3 | async-start | bytes 1048576 | tf_op jit(solution)/shard_map/all_to_all | solution.py:408
  51.7 0.0 collective-permute-start
  51.7 0.5 collective-permute-start.4
  52.2 1.0 collective-permute-done.received_ref
  53.2 0.1 add.2._.own_ref
  53.3 1.6 %collective-permute-start.1 = (bf16[256,512]{1,0:T(8,128)(2,1)S(1)}, bf16[256,512]{1,0:T(8,128)(2,1)S(1)}, u32[]{:S(2)}, u32[]{:S(2)}) collective-permute-start(bf16[256,512]{1,0:T(8,128)(2,1)S(1)} %add.2._.own_ref), channel_id=1, source_target_pairs={{0,2},{1,3},{2,0},{3,1},{4,6},{5,7},{6,4},{7,5},{8,10},{9,11},{10,... | collective-permute-start | bytes 786440 | tf_op jit(solution)/shard_map/ppermute | solution.py:412
  54.9 0.0 collective-permute-done.4.other_ref
  54.9 15.0 %backward.1.back_ref = bf16[256,1024]{1,0:T(8,128)(2,1)S(1)} custom-call(bf16[256,1024]{1,0:T(8,128)(2,1)S(1)} %bitcast.16, bf16[256,512]{1,0:T(8,128)(2,1)S(1)} %bitcast.23, bf16[256,512]{1,0:T(8,128)(2,1)S(1)} %collective-permute-done.4.other_ref, bf16[1024,1024]{1,0:T(8,128)(2,1)} %bitcast.25, bf16[1024,3072]{1,0:T(8,128)(2,1)} %wv_ref.3, ...), custom_call_target="tpu_custom_call" | custom-call | flops 4294967296 | bytes 13631488 | tf_op jit(solution)/shard_map/backward/pallas_call | solution.py:333
  69.8 0.0 collective-permute-done.1.received_ref
  69.9 1.0 add_mixed.1
  70.8 1.2 %all-to-all-done.3.own_ref = bf16[8,256,128]{2,1,0:T(8,128)(2,1)S(1)} async-done(((bf16[8,256,128]{2,1,0:T(8,128)(2,1)}), bf16[8,256,128]{2,1,0:T(8,128)(2,1)S(1)}, u32[]{:S(2)}, u32[]{:S(2)}) %all-to-all-start.3) | async-done | bytes 524320 | tf_op jit(solution)/shard_map/all_to_all | solution.py:408
  72.0 4.8 %all-to-all-start.2 = ((bf16[8,32,1536]{2,1,0:T(8,128)(2,1)}), bf16[8,32,1536]{2,1,0:T(8,128)(2,1)S(1)}, u32[]{:S(2)}, u32[]{:S(2)}) async-start(bf16[8,32,1536]{2,1,0:T(8,128)(2,1)} %bitcast.5), calls=%async_computation.2 | async-start | bytes 1572864 | tf_op jit(solution)/shard_map/all_to_all | solution.py:408
  76.8 0.0 copy-start
  76.8 0.1 collective-permute-start.6
  76.9 24.0 %all-to-all-done.2.in_ref.back_ref = bf16[8,32,1536]{2,1,0:T(8,128)(2,1)S(1)} async-done(((bf16[8,32,1536]{2,1,0:T(8,128)(2,1)}), bf16[8,32,1536]{2,1,0:T(8,128)(2,1)S(1)}, u32[]{:S(2)}, u32[]{:S(2)}) %all-to-all-start.2) | async-done | bytes 786464 | tf_op jit(solution)/shard_map/all_to_all | solution.py:408
  100.9 0.1 collective-permute-start.5
  101.0 0.0 collective-permute-done.6.other_ref
  101.0 0.0 all-gather.3.cloned.1.call-done
  101.0 0.0 copy-start.2
  101.1 1.6 %copy-done.2 = bf16[64,32,512]{2,1,0:T(8,128)(2,1)S(1)} copy-done((bf16[64,32,512]{2,1,0:T(8,128)(2,1)S(1)}, bf16[64,32,512]{2,1,0:T(8,128)(2,1)}, u32[]{:S(2)}) %copy-start.2) | copy-done | bytes 2097176
  102.6 0.0 copy-start.1
  102.6 0.0 copy-start.3
  102.6 0.7 mix_gradient.1
  103.4 0.5 collective-permute-start.7
  103.9 0.0 copy-done
  103.9 0.9 make_gradient.1
  104.8 0.0 collective-permute-done.5.other_ref
  104.8 0.0 copy-done.1
  104.8 0.0 copy-done.3
  104.8 1.0 make_output.1
  105.8 0.0 collective-permute-done.7.other_ref
  105.8 0.8 place.1
  (1 shorter events, 0.0 us)
Async XLA Ops:
  9.2 26.3 %copy-start.4 = (s32[2,16]{1,0:T(2,128)S(1)}, s32[2,16]{1,0:T(2,128)}, u32[]{:S(2)}) copy-start(s32[2,16]{1,0:T(2,128)} %mask_ref.1) | copy-start | bytes 388
  9.2 21.9 %all-to-all-start = ((bf16[8,32,1024]{2,1,0:T(8,128)(2,1)}), bf16[8,32,1024]{2,1,0:T(8,128)(2,1)S(1)}, u32[]{:S(2)}, u32[]{:S(2)}) async-start(bf16[8,32,1024]{2,1,0:T(8,128)(2,1)} %get-tuple-element.18), calls=%async_computation | async-start | bytes 1048576 | tf_op jit(solution)/shard_map/all_to_all | solution.py:408
  16.6 84.4 %all-gather.3.cloned.1.call-start = ((), (), s32[]{:S(2)}) async-start(), calls=%async_computation.4 | async-start | bytes 2359296 | tf_op jit(solution)/shard_map/all_gather | solution.py:490
  16.6 1.6 %collective-permute-start.2 = (bf16[8,32,512]{2,1,0:T(8,128)(2,1)S(1)}, bf16[8,32,512]{2,1,0:T(8,128)(2,1)S(1)}, u32[]{:S(2)}, u32[]{:S(2)}) collective-permute-start(bf16[8,32,512]{2,1,0:T(8,128)(2,1)S(1)} %get-tuple-element.22), channel_id=1, source_target_pairs={{0,1},{1,0},{2,3},{3,2},{4,5},{5,4},{6,7},{7,6},{8,9},{9,8},{10,11... | collective-permute-start | bytes 786440 | tf_op jit(solution)/shard_map/ppermute | solution.py:412
  18.3 8.4 %collective-permute-start.3 = (bf16[8,32,512]{2,1,0:T(8,128)(2,1)S(1)}, bf16[8,32,512]{2,1,0:T(8,128)(2,1)S(1)}, u32[]{:S(2)}, u32[]{:S(2)}) collective-permute-start(bf16[8,32,512]{2,1,0:T(8,128)(2,1)S(1)} %add.3.own_ref), channel_id=1, source_target_pairs={{0,2},{1,3},{2,0},{3,1},{4,6},{5,7},{6,4},{7,5},{8,10},{9,11},{10,... | collective-permute-start | bytes 786440 | tf_op jit(solution)/shard_map/ppermute | solution.py:412
  31.9 15.4 %all-to-all-start.1 = ((bf16[8,32,512]{2,1,0:T(8,128)(2,1)}), bf16[8,32,512]{2,1,0:T(8,128)(2,1)S(1)}, u32[]{:S(2)}, u32[]{:S(2)}) async-start(bf16[8,32,512]{2,1,0:T(8,128)(2,1)} %add_flow.1), calls=%async_computation.1 | async-start | bytes 524288 | tf_op jit(solution)/shard_map/all_to_all | solution.py:408
  47.3 24.7 %all-to-all-start.3 = ((bf16[8,256,128]{2,1,0:T(8,128)(2,1)}), bf16[8,256,128]{2,1,0:T(8,128)(2,1)S(1)}, u32[]{:S(2)}, u32[]{:S(2)}) async-start(bf16[8,256,128]{2,1,0:T(8,128)(2,1)} %get-tuple-element.30), calls=%async_computation.3 | async-start | bytes 1048576 | tf_op jit(solution)/shard_map/all_to_all | solution.py:408
  51.7 1.5 %collective-permute-start = (bf16[256,512]{1,0:T(8,128)(2,1)S(1)}, bf16[256,512]{1,0:T(8,128)(2,1)S(1)}, u32[]{:S(2)}, u32[]{:S(2)}) collective-permute-start(bf16[256,512]{1,0:T(8,128)(2,1)S(1)} %get-tuple-element.20), channel_id=1, source_target_pairs={{0,1},{1,0},{2,3},{3,2},{4,5},{5,4},{6,7},{7,6},{8,9},{9,8},{10,11... | collective-permute-start | bytes 786440 | tf_op jit(solution)/shard_map/ppermute | solution.py:412
  51.7 3.2 %collective-permute-start.4 = (bf16[256,512]{1,0:T(8,128)(2,1)S(1)}, bf16[256,512]{1,0:T(8,128)(2,1)S(1)}, u32[]{:S(2)}, u32[]{:S(2)}) collective-permute-start(bf16[256,512]{1,0:T(8,128)(2,1)S(1)} %bitcast.22), channel_id=1, source_target_pairs={{0,1},{1,0},{2,3},{3,2},{4,5},{5,4},{6,7},{7,6},{8,9},{9,8},{10,11... | collective-permute-start | bytes 786440 | tf_op jit(solution)/shard_map/ppermute | solution.py:412
  53.3 16.6 %collective-permute-start.1 = (bf16[256,512]{1,0:T(8,128)(2,1)S(1)}, bf16[256,512]{1,0:T(8,128)(2,1)S(1)}, u32[]{:S(2)}, u32[]{:S(2)}) collective-permute-start(bf16[256,512]{1,0:T(8,128)(2,1)S(1)} %add.2._.own_ref), channel_id=1, source_target_pairs={{0,2},{1,3},{2,0},{3,1},{4,6},{5,7},{6,4},{7,5},{8,10},{9,11},{10,... | collective-permute-start | bytes 786440 | tf_op jit(solution)/shard_map/ppermute | solution.py:412
  72.0 28.9 %all-to-all-start.2 = ((bf16[8,32,1536]{2,1,0:T(8,128)(2,1)}), bf16[8,32,1536]{2,1,0:T(8,128)(2,1)S(1)}, u32[]{:S(2)}, u32[]{:S(2)}) async-start(bf16[8,32,1536]{2,1,0:T(8,128)(2,1)} %bitcast.5), calls=%async_computation.2 | async-start | bytes 1572864 | tf_op jit(solution)/shard_map/all_to_all | solution.py:408
  76.8 27.1 %copy-start = (bf16[2,1,2,64,1024]{4,3,2,1,0:T(8,128)(2,1)S(1)}, bf16[2,1,2,64,1024]{4,3,2,1,0:T(8,128)(2,1)}, u32[]{:S(2)}) copy-start(bf16[2,1,2,64,1024]{4,3,2,1,0:T(8,128)(2,1)} %param.11) | copy-start | bytes 1572868
  76.8 24.2 %collective-permute-start.6 = (bf16[8,256,128]{2,1,0:T(8,128)(2,1)S(1)}, bf16[8,256,128]{2,1,0:T(8,128)(2,1)S(1)}, u32[]{:S(2)}, u32[]{:S(2)}) collective-permute-start(bf16[8,256,128]{2,1,0:T(8,128)(2,1)S(1)} %all-to-all-done.3.own_ref), channel_id=1, source_target_pairs={{0,1},{1,0},{2,3},{3,2},{4,5},{5,4},{6,7},{7,6},{8,9},{9,8},{10,11... | collective-permute-start | bytes 1572872 | tf_op jit(solution)/shard_map/ppermute | solution.py:412
  100.9 3.9 %collective-permute-start.5 = (bf16[8,32,512]{2,1,0:T(8,128)(2,1)S(1)}, bf16[8,32,512]{2,1,0:T(8,128)(2,1)S(1)}, u32[]{:S(2)}, u32[]{:S(2)}) collective-permute-start(bf16[8,32,512]{2,1,0:T(8,128)(2,1)S(1)} %cut_mixed.1.own_ref), channel_id=1, source_target_pairs={{0,1},{1,0},{2,3},{3,2},{4,5},{5,4},{6,7},{7,6},{8,9},{9,8},{10,11... | collective-permute-start | bytes 786440 | tf_op jit(solution)/shard_map/ppermute | solution.py:412
  101.0 1.6 %copy-start.2 = (bf16[64,32,512]{2,1,0:T(8,128)(2,1)S(1)}, bf16[64,32,512]{2,1,0:T(8,128)(2,1)}, u32[]{:S(2)}) copy-start(bf16[64,32,512]{2,1,0:T(8,128)(2,1)} %all-gather.3.cloned.1.call-done) | copy-start | bytes 6291460
  102.6 2.2 %copy-start.1 = (bf16[2,1,2,64,1024]{4,3,2,1,0:T(8,128)(2,1)S(1)}, bf16[2,1,2,64,1024]{4,3,2,1,0:T(8,128)(2,1)}, u32[]{:S(2)}) copy-start(bf16[2,1,2,64,1024]{4,3,2,1,0:T(8,128)(2,1)} %param.6) | copy-start | bytes 1572868
  102.6 2.2 %copy-start.3 = (f32[1,1024]{1,0:T(1,128)S(1)}, f32[1,1024]{1,0:T(1,128)}, u32[]{:S(2)}) copy-start(f32[1,1024]{1,0:T(1,128)} %gain_ref.3) | copy-start | bytes 12292
  103.4 2.4 %collective-permute-start.7 = (bf16[128,512]{1,0:T(8,128)(2,1)S(1)}, bf16[128,512]{1,0:T(8,128)(2,1)S(1)}, u32[]{:S(2)}, u32[]{:S(2)}) collective-permute-start(bf16[128,512]{1,0:T(8,128)(2,1)S(1)} %get-tuple-element.32), channel_id=1, source_target_pairs={{0,1},{1,0},{2,3},{3,2},{4,5},{5,4},{6,7},{7,6},{8,9},{9,8},{10,11... | collective-permute-start | bytes 393224 | tf_op jit(solution)/shard_map/ppermute | solution.py:412
Sparse Core Ops, SparseCore 0:
  32.0 55.9 all-gather.2
